TPU v7x, 256 devices: a whole 4x4x8 slice. The times are simulated.
256 devices in a mesh: slab: 32 (over z, x_lo, core), angle: 8 (over x_hi, y).
Axes of the slice: x: 4 (x_hi: 2, x_lo: 2; x = x_hi * 2 + x_lo), y: 4, z: 8, core: 2. Of those that a mesh axis runs over, the one named last changes fastest.
Arguments:
- volume: bfloat16 [2, 32, 128, 2048], P(None, 'slab'), may hold values from -1 to 1
- consensus: bfloat16 [2, 32, 128, 2048], P(None, 'slab'), may hold values from -3 to 3
- probe: bfloat16 [2, 128, 128], replicated, may hold values from -4.1875 to 4.1875
- intensities: bfloat16 [8, 128, 512, 128], P('angle', None, 'slab'), may hold values from 0 to 4
- positions: int32 [8, 512], P('angle', 'slab'), may hold values from 0 to 1920
- offsets: int32 [8, 32], P('angle', 'slab'), may hold values from 0 to 2047
Outputs:
- updated: float32 [2, 32, 128, 2048], P(None, 'slab')
All inputs are finite; a program needn't handle non-finite values.
Results may differ from a plain program's by a relative error of at most 0.0085.
Values may be sent and summed in bfloat16 or wider, within the bound.
A program may use at most 64 MiB of HBM per device.

v0:
```python
import math

import jax
import jax.numpy as jnp
from jax import lax
from jax.sharding import PartitionSpec as P

mix_weight = 0.5


def dft_tables(length):
    indices = jnp.arange(length, dtype=jnp.int32)
    phases = (indices[:, None] * indices[None, :] % length).astype(jnp.float32) * (
        2.0 * math.pi / length
    )
    factor = 1.0 / math.sqrt(length)
    real_t = (jnp.cos(phases) * factor).astype(jnp.bfloat16)
    imag_t = (-jnp.sin(phases) * factor).astype(jnp.bfloat16)
    right_fwd = jnp.concatenate(
        [jnp.concatenate([real_t, imag_t], axis=1), jnp.concatenate([-imag_t, real_t], axis=1)],
        axis=0,
    )
    right_inv = jnp.concatenate(
        [jnp.concatenate([real_t, -imag_t], axis=1), jnp.concatenate([imag_t, real_t], axis=1)],
        axis=0,
    )
    return (real_t, imag_t, right_fwd, right_inv)


def wave_grad(patch, probe, measured, tables):
    real_t, imag_t, right_fwd, right_inv = tables
    width = probe.shape[-1]
    probe_re = probe[0].astype(jnp.float32)[:, None, :]
    probe_im = probe[1].astype(jnp.float32)[:, None, :]
    patch_re = patch[0].astype(jnp.float32)
    patch_im = patch[1].astype(jnp.float32)
    exit_wave = jnp.concatenate(
        [probe_re * patch_re - probe_im * patch_im, probe_re * patch_im + probe_im * patch_re],
        axis=-1,
    ).astype(jnp.bfloat16)
    half = jnp.einsum(
        "jbk,kc->jbc", exit_wave, right_fwd, preferred_element_type=jnp.float32
    ).astype(jnp.bfloat16)
    first = jnp.einsum("ij,jbc->ibc", real_t, half, preferred_element_type=jnp.float32)
    second = jnp.einsum("ij,jbc->ibc", imag_t, half, preferred_element_type=jnp.float32)
    far_re = first[..., :width] - second[..., width:]
    far_im = first[..., width:] + second[..., :width]
    misfit = far_re * far_re + far_im * far_im - measured.astype(jnp.float32)
    residual_wave = jnp.concatenate([misfit * far_re, misfit * far_im], axis=-1).astype(
        jnp.bfloat16
    )
    back_half = jnp.einsum(
        "jbk,kc->jbc", residual_wave, right_inv, preferred_element_type=jnp.float32
    ).astype(jnp.bfloat16)
    first = jnp.einsum("ij,jbc->ibc", real_t, back_half, preferred_element_type=jnp.float32)
    second = jnp.einsum("ij,jbc->ibc", imag_t, back_half, preferred_element_type=jnp.float32)
    grad_re = first[..., :width] + second[..., width:]
    grad_im = first[..., width:] - second[..., :width]
    return jnp.stack(
        [probe_re * grad_re + probe_im * grad_im, probe_re * grad_im - probe_im * grad_re]
    )


def per_device(volume, consensus, probe, intensities, positions, offsets):
    row_count = volume.shape[2]
    col_count = volume.shape[3]
    angle_count = offsets.shape[0]
    pos_count = positions.shape[1]
    patch_width = probe.shape[-1]
    slab_devices = lax.axis_size("slab")
    angle_devices = lax.axis_size("angle")
    tables = dft_tables(patch_width)
    angle_local = 0
    depth = 0
    total = jnp.roll(volume[:, depth].astype(jnp.float32), -offsets[angle_local, depth], axis=-1)
    partials = [total]
    partial_value = jnp.stack(partials, axis=1)
    summed = lax.psum_scatter(partial_value, "slab", scatter_dimension=3, tiled=True).astype(
        jnp.bfloat16
    )
    projection = lax.all_gather(summed, "slab", axis=3, tiled=True)
    angle_local = 0
    proj_now = projection[:, angle_local]
    pos_row = positions[angle_local]
    starts = [pos_row[item] for item in range(pos_count)]
    patch = jnp.stack(
        [
            lax.dynamic_slice_in_dim(proj_now, starts[item], patch_width, 2)
            for item in range(pos_count)
        ],
        axis=2,
    )
    grads = wave_grad(patch, probe, intensities[angle_local], tables)
    total = jnp.zeros((2, row_count, col_count), jnp.float32)
    for item in range(pos_count):
        window = lax.dynamic_slice_in_dim(total, starts[item], patch_width, 2)
        total = lax.dynamic_update_slice_in_dim(total, window + grads[:, :, item], starts[item], 2)
    grads_all = [total]
    detector_grad = lax.psum(jnp.stack(grads_all, axis=1), "slab")
    depth = 0
    angle_local = 0
    total = jnp.roll(detector_grad[:, angle_local], offsets[angle_local, depth], axis=-1)
    slices = [total]
    volume_grad = jnp.stack(slices, axis=1)
    total_pos = pos_count * slab_devices
    total_angles = angle_count * angle_devices
    rate = math.sqrt(col_count / (total_pos * total_angles * row_count))
    summed_grad = lax.psum(volume_grad, "angle")
    current = volume.astype(jnp.float32)
    result = current - rate * summed_grad - mix_weight * (current - consensus.astype(jnp.float32))
    return result


def solution(mesh):
    return jax.shard_map(
        per_device,
        mesh=mesh,
        in_specs=(
            P(None, "slab", None, None),
            P(None, "slab", None, None),
            P(),
            P("angle", None, "slab", None),
            P("angle", "slab"),
            P("angle", "slab"),
        ),
        out_specs=P(None, "slab", None, None),
        check_vma=False,
    )
```

profile of v0, /device:TPU:1, one launch (start us, length us, event | category | flops | bytes accessed | tf_op | source)
XLA Modules:
  0.0 608.6 jit_solution(978176647007519732)
XLA Ops:
  7.2 1.5 convert_bitcast_fusion
  8.7 2.5 fusion.4
  11.2 2.8 copy.23
  14.0 130.4 %all-reduce.8 = bf16[2,1,128,2048]{2,0,1,3:T(2,128)(2,1)S(1)} all-reduce(f32[2,1,128,2048]{2,0,1,3:T(2,128)S(1)} %bitcast.171), channel_id=2, replica_groups=mesh['slab'=32,'angle'=8] {'slab'}, use_global_device_ids=true, to_apply=%region_0.2.clone | all-reduce | flops 524288 | bytes 3145728
  145.7 0.6 dynamic-slice_convert_fusion
  146.4 0.7 fusion.80
  177.7 34.2 %all-gather.2.cloned.1.call-done = bf16[2,1,128,2048]{2,0,1,3:T(2,128)(2,1)} async-done(((bf16[2,1,128,64]{2,0,1,3:T(2,128)(2,1)}), bf16[2,1,128,2048]{2,0,1,3:T(2,128)(2,1)}) %all-gather.2.cloned.1.call-update) | async-done | bytes 1048592 | tf_op jit(solution)/shard_map/all_gather | solution.py:81
  211.9 2.3 constant_dynamic-slice_fusion
  217.4 0.6 fusion.51
  218.0 0.6 fusion.55
  219.9 0.6 fusion.49
  220.6 0.6 fusion.53
  221.6 1.6 broadcast_in_dim.2
  223.2 2.0 dynamic_update_slice.49
  225.2 1.0 bitcast_add_fusion.13
  226.3 2.0 dynamic_update_slice.50
  228.3 1.0 bitcast_add_fusion.12
  229.3 2.0 dynamic_update_slice.51
  231.4 1.0 bitcast_add_fusion.11
  232.4 2.0 dynamic_update_slice.52
  234.5 1.0 bitcast_add_fusion.10
  235.5 2.0 dynamic_update_slice.53
  237.6 1.0 bitcast_add_fusion.9
  238.6 2.0 dynamic_update_slice.54
  240.7 1.0 bitcast_add_fusion.8
  241.7 2.0 dynamic_update_slice.55
  243.7 1.0 bitcast_add_fusion.7
  244.8 2.0 dynamic_update_slice.56
  246.8 1.0 bitcast_add_fusion.6
  247.9 2.0 dynamic_update_slice.57
  249.9 1.0 bitcast_add_fusion.5
  251.0 2.0 dynamic_update_slice.58
  253.0 1.0 bitcast_add_fusion.4
  254.1 2.0 dynamic_update_slice.59
  256.1 1.0 bitcast_add_fusion.3
  257.2 2.0 dynamic_update_slice.60
  259.2 1.0 bitcast_add_fusion.2
  260.3 2.0 dynamic_update_slice.61
  262.3 1.0 bitcast_add_fusion.1
  263.3 2.0 dynamic_update_slice.62
  265.4 1.0 bitcast_add_fusion
  266.4 2.0 dynamic_update_slice.63
  268.5 1.0 fusion.37
  269.5 2.0 dynamic_update_slice.65
  271.7 229.8 %all-reduce.5.cloned.1.call-done = f32[2,128,2048]{2,1,0:T(8,128)} async-done(((f32[2,128,2048]{2,1,0:T(8,128)}), f32[2,128,2048]{2,1,0:T(8,128)}) %all-reduce.5.cloned.1.call-update) | async-done | bytes 2097168 | tf_op jit(solution)/shard_map/psum | solution.py:99
  501.5 4.0 fusion.3
  505.6 93.1 %all-reduce.7.cloned.1.call-done = f32[2,1,128,2048]{3,2,1,0:T(8,128)} async-done(((f32[2,1,128,2048]{3,2,1,0:T(8,128)}), f32[2,1,128,2048]{3,2,1,0:T(8,128)}) %all-reduce.7.cloned.1.call-update) | async-done | bytes 2097168 | tf_op jit(solution)/shard_map/psum | solution.py:108
  598.7 3.4 fusion
  (60 shorter events, 6.0 us)
Async XLA Ops:
  6.5 205.4 %all-gather.2.cloned.1.call-start = ((), (), s32[]{:S(2)}) async-start(), calls=%async_computation | async-start | bytes 1081344 | tf_op jit(solution)/shard_map/all_gather | solution.py:81
  14.0 130.4 %copy-start.5 = (u32[256]{0:T(256)S(1)}, u32[256]{0:T(256)}, u32[]{:S(2)}) copy-start(u32[256]{0:T(256)} %constant.70) | copy-start | bytes 3076
  14.0 132.4 %copy-start.3 = (s32[1,16]{1,0:T(1,128)S(1)}, s32[1,16]{1,0:T(1,128)}, u32[]{:S(2)}) copy-start(s32[1,16]{1,0:T(1,128)} %param.12) | copy-start | bytes 196
  14.0 163.7 %copy-start.4 = (bf16[2,128,128]{2,1,0:T(8,128)(2,1)S(1)}, bf16[2,128,128]{2,1,0:T(8,128)(2,1)}, u32[]{:S(2)}) copy-start(bf16[2,128,128]{2,1,0:T(8,128)(2,1)} %param.10) | copy-start | bytes 196612
  146.3 355.2 %all-reduce.5.cloned.1.call-start = ((), (), s32[]{:S(2)}) async-start(), calls=%async_computation.1 | async-start | bytes 4194304 | tf_op jit(solution)/shard_map/psum | solution.py:99
  218.0 1.0 copy-start.2
  271.6 327.1 %all-reduce.7.cloned.1.call-start = ((), (), s32[]{:S(2)}) async-start(), calls=%async_computation.2 | async-start | bytes 4194304 | tf_op jit(solution)/shard_map/psum | solution.py:108
  505.6 93.1 %copy-start = (bf16[2,1,128,2048]{3,2,1,0:T(8,128)(2,1)S(1)}, bf16[2,1,128,2048]{3,2,1,0:T(8,128)(2,1)}, u32[]{:S(2)}) copy-start(bf16[2,1,128,2048]{3,2,1,0:T(8,128)(2,1)} %param.8) | copy-start | bytes 3145732
  505.6 93.1 %copy-start.1 = (bf16[2,1,128,2048]{3,2,1,0:T(8,128)(2,1)S(1)}, bf16[2,1,128,2048]{3,2,1,0:T(8,128)(2,1)}, u32[]{:S(2)}) copy-start(bf16[2,1,128,2048]{3,2,1,0:T(8,128)(2,1)} %param.9) | copy-start | bytes 3145732
Sparse Core Ops, SparseCore 0:
  146.5 65.3 all-gather.1
  271.7 229.7 all-reduce.4
  505.7 92.9 all-reduce.6
where the time goes:
time: 614 us; the launch traced here: 609 us
  waiting for transfers between devices  357 us (58%)
  blocking collectives  130 us (21%)
  between operations  45 us (7%)
  local copies, waits for them, and re-layouts  43.8 us (7%)
  other arithmetic  28.8 us (5%)
    psum x1, waiting for transfers between devices, per_device(): detector_grad = lax.psum(jnp.stack(grads_all, axis=1), 'slab')  230 us
    unnamed x1, blocking collectives  130 us
    psum x1, waiting for transfers between devices, per_device(): summed_grad = lax.psum(volume_grad, 'angle')  93.1 us
    all_gather x1, waiting for transfers between devices, per_device(): projection = lax.all_gather(summed, 'slab', axis=3, tiled=True)  34.2 us
    dynamic_update_slice x16, local copies, waits for them, and re-layouts, per_device(): lax.dynamic_update_slice_in_dim(total, window + grads[:, :, item], starts...  32.6 us
    add x15, other arithmetic, per_device(): window + grads[:, :, item]  15.7 us
  transfers between devices with their start and end apart: 3, of which 3 were waited for; matrix products, arithmetic and copies ran while one was open for 0% of the time, Pallas kernels for 0%

commit v1 on v0

v1 whole, which is shorter than its diff:
```python
import math

import jax
import jax.numpy as jnp
import ml_dtypes
import numpy as np
from jax import lax
from jax.experimental import pallas as pl
from jax.experimental.pallas import tpu as pltpu
from jax.sharding import PartitionSpec as P

MIX = 0.5
NX = 2048
PW = 128
LANES = 128
TILES = NX // LANES
NZC = 8
NXL = 2
NXH = 2
NY = 4
ANGLES = NXH * NY
BLOCK = 16
HALF = NX // 2
CHUNK = NX // NY
FAR_FIRST = (4, 3, 5, 2, 6, 1, 7, 0)
VMEM = 48 * 1024 * 1024


def dft_tables():
    indices = np.arange(PW, dtype=np.int64)
    phases = (indices[:, None] * indices[None, :] % PW).astype(np.float64) * (2.0 * math.pi / PW)
    factor = 1.0 / math.sqrt(PW)
    re = (np.cos(phases) * factor).astype(ml_dtypes.bfloat16)
    im = (-np.sin(phases) * factor).astype(ml_dtypes.bfloat16)
    forward = np.block([[re, im], [-im, re]])
    inverse = np.block([[re, -im], [im, re]])
    return forward.astype(ml_dtypes.bfloat16), inverse.astype(ml_dtypes.bfloat16)


class Here:
    def __init__(self):
        s = lax.axis_index("slab")
        a = lax.axis_index("angle")
        self.a = a
        self.c = lax.rem(s, 2)
        self.xl = lax.rem(lax.div(s, 2), 2)
        self.zc = lax.div(s, 4)
        self.y = lax.rem(a, NY)
        self.xh = lax.div(a, NY)
        self.m = self.xl * NZC + self.zc

    def z_of(self, rel):
        return lax.rem(self.zc + rel, NZC)

    def y_of(self, rel):
        return lax.rem(self.y + rel, NY)

    def x_of(self, flip):
        return 1 - self.xl if flip else self.xl

    def chip(self, rel_z, flip_x):
        return self.device(zc=self.z_of(rel_z), xl=self.x_of(flip_x))

    def angle_peer(self, flip_xh, rel_y):
        return self.device(xh=1 - self.xh if flip_xh else self.xh, y=self.y_of(rel_y))

    def device(self, zc=None, xl=None, c=None, xh=None, y=None):
        zc = self.zc if zc is None else zc
        xl = self.xl if xl is None else xl
        c = self.c if c is None else c
        xh = self.xh if xh is None else xh
        y = self.y if y is None else y
        return {"slab": zc * 4 + xl * 2 + c, "angle": xh * NY + y}

    @property
    def sibling(self):
        return self.device(c=1 - self.c)

    def greet(self):
        peers = [self.sibling]
        peers += [self.chip(r, f) for f in (0, 1) for r in range(NZC) if r or f]
        peers += [self.angle_peer(f, r) for f in (0, 1) for r in range(NY) if r or f]
        barrier = pltpu.get_barrier_semaphore()
        for peer in peers:
            pl.semaphore_signal(barrier, 1, device_id=peer, device_id_type=pl.DeviceIdType.MESH)
        pl.semaphore_wait(barrier, len(peers))


def rows16(block):
    return pl.ds(pl.multiple_of(block * BLOCK, BLOCK), BLOCK)


def half_cols(core):
    return pl.ds(pl.multiple_of(core * HALF, HALF), HALF)


def chunk_cols(y):
    return pl.ds(pl.multiple_of(y * CHUNK, CHUNK), CHUNK)


def remote(src, dst, send, recv, to):
    return pltpu.make_async_remote_copy(
        src_ref=src,
        dst_ref=dst,
        send_sem=send,
        recv_sem=recv,
        device_id=to,
        device_id_type=pl.DeviceIdType.MESH,
    )


def shifted_tiles(load, start, count):
    x = load(slice(None)).astype(jnp.float32)
    x = pltpu.roll(x, lax.rem(NX - start, NX), 1)
    return [x[:, j * LANES : (j + 1) * LANES] for j in range(count)]


def ring_quarters(here, piece, arrived, sems, order):
    s_up, s_dn, s_on, r_dn, r_up, r_on = sems
    up = here.angle_peer(0, 1)
    dn = here.angle_peer(0, NY - 1)
    y, y_dn, y_up, y_far = here.y, here.y_of(NY - 1), here.y_of(1), here.y_of(2)
    sent = []

    def start(src, dst, send, recv, to):
        copy = remote(src, dst, send, recv, to)
        copy.start()
        sent.append(copy)

    def onward(k):
        rel = order[k]
        if k % 2 == 0:
            remote(piece(rel, y_dn), piece(rel, y_dn), s_on.at[rel], r_dn.at[rel], up).wait_recv()
            start(piece(rel, y_dn), piece(rel, y_dn), s_on.at[rel], r_on.at[rel], up)
        else:
            remote(piece(rel, y_up), piece(rel, y_up), s_on.at[rel], r_up.at[rel], dn).wait_recv()
            start(piece(rel, y_up), piece(rel, y_up), s_on.at[rel], r_on.at[rel], dn)

    for k, rel in enumerate(order):
        arrived(rel)
        start(piece(rel, y), piece(rel, y), s_up.at[rel], r_dn.at[rel], up)
        start(piece(rel, y), piece(rel, y), s_dn.at[rel], r_up.at[rel], dn)
        if k >= 1:
            onward(k - 1)
    onward(len(order) - 1)

    def finish(k):
        rel = order[k]
        if k % 2 == 0:
            remote(piece(rel, y_up), piece(rel, y_up), s_on.at[rel], r_up.at[rel], dn).wait_recv()
        else:
            remote(piece(rel, y_dn), piece(rel, y_dn), s_on.at[rel], r_dn.at[rel], up).wait_recv()
        remote(piece(rel, y_far), piece(rel, y_far), s_on.at[rel], r_on.at[rel], up).wait_recv()

    return finish, sent


def project_kernel(
    vol, off, proj, offs_out, gath, acc, sib, offt, offv, offs_s,
    s_off, r_off, s_t1, r_t1, s_up, s_dn, s_on, r_dn, r_up, r_on,
    s_sib, r_sib, s_z, r_z, s_x, r_x, s_c, r_c, s_oa, r_oa, l_sem,
):
    here = Here()
    here.greet()
    sent = []

    def start(src, dst, send, recv, to):
        copy = remote(src, dst, send, recv, to)
        copy.start()
        sent.append(copy)

    cols = chunk_cols(here.y)
    for r in FAR_FIRST:
        for f in (0, 1):
            if not (r or f):
                continue
            slot = (NZC - r) % NZC
            to = here.chip(r, f)
            start(off, offt.at[here.m], s_off.at[f, r], r_off.at[f, slot], to)
            block = here.x_of(f) * NZC + here.z_of(r)
            start(vol.at[rows16(block), cols], gath.at[f, slot, :, cols], s_t1.at[f, r], r_t1.at[f, slot], to)
    offt[here.m] = off[...]
    gath[0, 0] = vol[rows16(here.m), :]
    acc[...] = jnp.zeros_like(acc)

    def piece(rel, y):
        if rel == 0:
            return gath.at[1, 0, :, chunk_cols(y)]
        return gath.at[:, rel, :, chunk_cols(y)]

    def arrived(rel):
        for f in (0, 1):
            if rel or f:
                part = gath.at[f, rel, :, cols]
                remote(part, part, s_t1.at[f, rel], r_t1.at[f, rel], here.chip(rel, f)).wait_recv()

    order = tuple((NZC - r) % NZC for r in FAR_FIRST)
    finish, ring_sent = ring_quarters(here, piece, arrived, (s_up, s_dn, s_on, r_dn, r_up, r_on), order)
    sent += ring_sent

    for f in (0, 1):
        for r in range(NZC):
            if r or f:
                part = offt.at[here.x_of(f) * NZC + here.z_of(r)]
                remote(part, part, s_off.at[f, r], r_off.at[f, r], here.chip(r, f)).wait_recv()
    for g in range(NXL * NZC):
        offv[g : g + 1, :] = offt[g, 0:1, :]
    for f in (0, 1):
        for r in range(NY):
            if r or f:
                back = (NY - r) % NY
                start(offv, offs_out.at[here.a], s_oa.at[f, r], r_oa.at[f, back], here.angle_peer(f, r))
    offs_out[here.a] = offv[...]
    down = pltpu.make_async_copy(offv, offs_s, l_sem)
    down.start()
    down.wait()

    for k in range(NZC):
        finish(k)

    def add_slot(i, carry):
        f = lax.div(i, NZC)
        rel = lax.rem(i, NZC)
        g = lax.rem(here.xl + f, NXL) * NZC + here.z_of(rel)
        tiles = shifted_tiles(lambda where: gath[f, rel, :, where], offs_s[g, 0], TILES)
        for j, tile in enumerate(tiles):
            acc[:, j * LANES : (j + 1) * LANES] += tile
        return carry

    lax.fori_loop(0, NXL * NZC, add_slot, 0)

    mine, other = half_cols(here.c), half_cols(1 - here.c)
    start(acc.at[:, other], sib, s_sib, r_sib, here.sibling)
    remote(sib, sib, s_sib, r_sib, here.sibling).wait_recv()
    proj[rows16(here.m), mine] = (acc[:, mine] + sib[...]).astype(jnp.bfloat16)

    own = proj.at[rows16(here.m), mine]
    for r in FAR_FIRST[:-1]:
        start(own, own, s_z.at[r], r_z.at[(NZC - r) % NZC], here.chip(r, 0))
    start(own, own, s_x.at[0], r_x.at[0], here.chip(0, 1))
    start(own, own, s_c.at[0, 0], r_c.at[0, 0], here.sibling)
    for rel in (1, 7, 2, 6, 3, 5, 4):
        got = proj.at[rows16(here.xl * NZC + here.z_of(rel)), mine]
        remote(got, got, s_z.at[rel], r_z.at[rel], here.chip(rel, 0)).wait_recv()
        start(got, got, s_x.at[rel], r_x.at[rel], here.chip(0, 1))
        start(got, got, s_c.at[0, rel], r_c.at[0, rel], here.sibling)
    for rel in (0, 1, 7, 2, 6, 3, 5, 4):
        got = proj.at[rows16(here.x_of(1) * NZC + here.z_of(rel)), mine]
        remote(got, got, s_x.at[rel], r_x.at[rel], here.chip(0, 1)).wait_recv()
        start(got, got, s_c.at[1, rel], r_c.at[1, rel], here.sibling)
    for f in (0, 1):
        for rel in (0, 1, 7, 2, 6, 3, 5, 4):
            got = proj.at[rows16(here.x_of(f) * NZC + here.z_of(rel)), other]
            remote(got, got, s_c.at[f, rel], r_c.at[f, rel], here.sibling).wait_recv()
    for f in (0, 1):
        for r in range(NY):
            if r or f:
                a_from = (1 - here.xh if f else here.xh) * NY + here.y_of(r)
                part = offs_out.at[a_from]
                remote(part, part, s_oa.at[f, r], r_oa.at[f, r], here.angle_peer(f, r)).wait_recv()
    for copy in sent:
        copy.wait_send()


def wave_kernel(proj, probe, measured, pos, forward, inverse, out, total):
    total[...] = jnp.zeros_like(total)
    pairs = measured.shape[1] // (2 * PW)

    def one_pair(pair, carry):
        p_re = probe[0].astype(jnp.float32)
        p_im = probe[1].astype(jnp.float32)
        fwd = forward[...]
        inv = inverse[...]
        starts = []
        exits = []
        for k in range(2):
            at = pos[2 * pair + k]
            first = jnp.minimum(lax.div(at, LANES), TILES - 2)
            inner = at - first * LANES
            where = pl.ds(pl.multiple_of(first * LANES, LANES), 2 * LANES)
            starts.append((where, inner))
            row = lax.broadcasted_iota(jnp.int32, (2 * LANES, PW), 0)
            col = lax.broadcasted_iota(jnp.int32, (2 * LANES, PW), 1)
            pick = jnp.where(row == col + inner, 1.0, 0.0).astype(jnp.bfloat16)
            patch = jnp.dot(proj[:, where], pick, preferred_element_type=jnp.float32)
            re, im = patch[:PW], patch[PW:]
            exits.append(
                jnp.concatenate([p_re * re - p_im * im, p_re * im + p_im * re], axis=1).astype(jnp.bfloat16)
            )
        half = jnp.dot(jnp.concatenate(exits, axis=0), fwd, preferred_element_type=jnp.float32).astype(jnp.bfloat16)
        half = jnp.concatenate(
            [
                jnp.concatenate([half[:PW, :PW], half[PW:, :PW]], axis=1),
                jnp.concatenate([half[:PW, PW:], half[PW:, PW:]], axis=1),
            ],
            axis=0,
        )
        far = jnp.dot(inv, half, preferred_element_type=jnp.float32)
        f_re, f_im = far[:PW], far[PW:]
        target = measured[:, pl.ds(pl.multiple_of(pair * 2 * PW, 2 * PW), 2 * PW)].astype(jnp.float32)
        misfit = f_re * f_re + f_im * f_im - target
        w_re = (misfit * f_re).astype(jnp.bfloat16)
        w_im = (misfit * f_im).astype(jnp.bfloat16)
        wave = jnp.concatenate(
            [
                jnp.concatenate([w_re[:, :PW], w_im[:, :PW]], axis=1),
                jnp.concatenate([w_re[:, PW:], w_im[:, PW:]], axis=1),
            ],
            axis=0,
        )
        back = jnp.dot(wave, inv, preferred_element_type=jnp.float32).astype(jnp.bfloat16)
        back = jnp.concatenate(
            [
                jnp.concatenate([back[:PW, :PW], back[PW:, :PW]], axis=1),
                jnp.concatenate([back[:PW, PW:], back[PW:, PW:]], axis=1),
            ],
            axis=0,
        )
        grad = jnp.dot(fwd, back, preferred_element_type=jnp.float32)
        for k, (where, inner) in enumerate(starts):
            g_re = grad[:PW, k * PW : (k + 1) * PW]
            g_im = grad[PW:, k * PW : (k + 1) * PW]
            patch_grad = jnp.concatenate(
                [p_re * g_re + p_im * g_im, p_re * g_im - p_im * g_re], axis=0
            ).astype(jnp.bfloat16)
            row = lax.broadcasted_iota(jnp.int32, (PW, 2 * LANES), 0)
            col = lax.broadcasted_iota(jnp.int32, (PW, 2 * LANES), 1)
            put = jnp.where(col == row + inner, 1.0, 0.0).astype(jnp.bfloat16)
            total[:, where] += jnp.dot(patch_grad, put, preferred_element_type=jnp.float32)
        return carry

    lax.fori_loop(0, pairs, one_pair, 0)
    out[...] = total[...].astype(jnp.bfloat16)


def volume_kernel(
    part, offs, out, cbuf, xsend, xbuf, zsend, zbuf, dgall, vsend,
    s_c, r_c, s_x, r_x, s_z, r_z, s_a, r_a, s_s, r_s,
    s_v, r_v, s_up, s_dn, s_on, r_dn, r_up, r_on,
):
    here = Here()
    here.greet()
    sent = []

    def start(src, dst, send, recv, to):
        copy = remote(src, dst, send, recv, to)
        copy.start()
        sent.append(copy)

    mine, other = half_cols(here.c), half_cols(1 - here.c)
    for f in (1, 0):
        for r in FAR_FIRST:
            src = part.at[rows16(here.x_of(f) * NZC + here.z_of(r)), other]
            start(src, cbuf.at[f, r], s_c.at[f, r], r_c.at[f, r], here.sibling)
    for r in FAR_FIRST:
        got = cbuf.at[1, r]
        remote(got, got, s_c.at[1, r], r_c.at[1, r], here.sibling).wait_recv()
        own = part[rows16(here.x_of(1) * NZC + here.z_of(r)), mine]
        xsend[r] = (own.astype(jnp.float32) + got[...].astype(jnp.float32)).astype(jnp.bfloat16)
        start(xsend.at[r], xbuf.at[r], s_x.at[r], r_x.at[r], here.chip(0, 1))
    total = None
    for r in FAR_FIRST:
        got = cbuf.at[0, r]
        remote(got, got, s_c.at[0, r], r_c.at[0, r], here.sibling).wait_recv()
        remote(xbuf.at[r], xbuf.at[r], s_x.at[r], r_x.at[r], here.chip(0, 1)).wait_recv()
        own = part[rows16(here.xl * NZC + here.z_of(r)), mine]
        value = own.astype(jnp.float32) + got[...].astype(jnp.float32) + xbuf[r].astype(jnp.float32)
        if r:
            zsend[r] = value.astype(jnp.bfloat16)
            slot = (NZC - r) % NZC
            start(zsend.at[r], zbuf.at[slot], s_z.at[r], r_z.at[slot], here.chip(r, 0))
        else:
            total = value
    for r in range(1, NZC):
        remote(zbuf.at[r], zbuf.at[r], s_z.at[r], r_z.at[r], here.chip(r, 0)).wait_recv()
        total = total + zbuf[r].astype(jnp.float32)
    dgall[here.a, :, mine] = total.astype(jnp.bfloat16)
    own = dgall.at[here.a, :, mine]
    peers = [(0, 2), (1, 2), (1, 1), (1, 3), (0, 1), (0, 3), (1, 0)]
    for f, r in peers:
        start(own, own, s_a.at[f, r], r_a.at[f, (NY - r) % NY], here.angle_peer(f, r))
    start(own, own, s_s.at[0, 0], r_s.at[0, 0], here.sibling)

    def angle_of(f, r):
        return (1 - here.xh if f else here.xh) * NY + here.y_of(r)

    for f, r in reversed(peers):
        got = dgall.at[angle_of(f, r), :, mine]
        remote(got, got, s_a.at[f, r], r_a.at[f, r], here.angle_peer(f, r)).wait_recv()
        start(got, got, s_s.at[f, r], r_s.at[f, r], here.sibling)
    for f, r in [(0, 0)] + peers:
        got = dgall.at[angle_of(f, r), :, other]
        remote(got, got, s_s.at[f, r], r_s.at[f, r], here.sibling).wait_recv()

    cols = chunk_cols(here.y)

    def gradient(f, r):
        g = here.x_of(f) * NZC + here.z_of(r)
        sums = [jnp.zeros((BLOCK, LANES), jnp.float32)] * (CHUNK // LANES)

        def add_angle(b, sums):
            first = lax.rem(here.y * CHUNK + NX - offs[b * NXL * NZC + g, 0], NX)
            tiles = shifted_tiles(lambda where: dgall[b, :, where], first, CHUNK // LANES)
            return [x + t for x, t in zip(sums, tiles)]

        sums = lax.fori_loop(0, ANGLES, add_angle, sums)
        return jnp.concatenate(sums, axis=1).astype(jnp.bfloat16)

    for r in FAR_FIRST:
        for f in (0, 1):
            value = gradient(f, r)
            if r or f:
                slot = (NZC - r) % NZC
                vsend[f, r] = value
                start(
                    vsend.at[f, r],
                    out.at[here.xl, rows16(here.zc), cols],
                    s_v.at[f, r],
                    r_v.at[f, slot],
                    here.chip(r, f),
                )
            else:
                out[here.xl, rows16(here.zc), cols] = value

    def piece(rel, y):
        return out.at[:, rows16(here.z_of(rel)), chunk_cols(y)]

    def arrived(rel):
        for f in (0, 1):
            if rel or f:
                got = out.at[here.x_of(f), rows16(here.z_of(rel)), cols]
                remote(got, got, s_v.at[f, rel], r_v.at[f, rel], here.chip(rel, f)).wait_recv()

    order = tuple((NZC - r) % NZC for r in FAR_FIRST)
    finish, ring_sent = ring_quarters(here, piece, arrived, (s_up, s_dn, s_on, r_dn, r_up, r_on), order)
    sent += ring_sent
    for k in range(NZC):
        finish(k)
    for copy in sent:
        copy.wait_send()


def dma(*shape):
    return pltpu.SemaphoreType.DMA(shape)


def vmem():
    return pl.BlockSpec(memory_space=pltpu.VMEM)


def smem():
    return pl.BlockSpec(memory_space=pltpu.SMEM)


def project(lines, off):
    return pl.pallas_call(
        project_kernel,
        out_shape=(
            jax.ShapeDtypeStruct((2 * PW, NX), jnp.bfloat16),
            jax.ShapeDtypeStruct((ANGLES, NXL * NZC, LANES), jnp.int32),
        ),
        in_specs=[vmem(), vmem()],
        out_specs=(vmem(), vmem()),
        scratch_shapes=[
            pltpu.VMEM((NXL, NZC, BLOCK, NX), jnp.bfloat16),
            pltpu.VMEM((BLOCK, NX), jnp.float32),
            pltpu.VMEM((BLOCK, HALF), jnp.float32),
            pltpu.VMEM((NXL * NZC, 8, LANES), jnp.int32),
            pltpu.VMEM((NXL * NZC, LANES), jnp.int32),
            pltpu.SMEM((NXL * NZC, LANES), jnp.int32),
            dma(NXL, NZC), dma(NXL, NZC), dma(NXL, NZC), dma(NXL, NZC),
            dma(NZC), dma(NZC), dma(NZC), dma(NZC), dma(NZC), dma(NZC),
            pltpu.SemaphoreType.DMA, pltpu.SemaphoreType.DMA,
            dma(NZC), dma(NZC), dma(NZC), dma(NZC),
            dma(NXL, NZC), dma(NXL, NZC),
            dma(NXH, NY), dma(NXH, NY),
            pltpu.SemaphoreType.DMA,
        ],
        compiler_params=pltpu.CompilerParams(collective_id=0, has_side_effects=True, vmem_limit_bytes=VMEM),
        name="project",
    )(lines, off)


def waves(proj, probe, measured, pos, forward, inverse):
    return pl.pallas_call(
        wave_kernel,
        out_shape=jax.ShapeDtypeStruct((2 * PW, NX), jnp.bfloat16),
        in_specs=[vmem(), vmem(), vmem(), smem(), vmem(), vmem()],
        out_specs=vmem(),
        scratch_shapes=[pltpu.VMEM((2 * PW, NX), jnp.float32)],
        compiler_params=pltpu.CompilerParams(vmem_limit_bytes=VMEM),
        name="waves",
    )(proj, probe, measured, pos, forward, inverse)


def volume_gradient(part, offs):
    bf16 = jnp.bfloat16
    return pl.pallas_call(
        volume_kernel,
        out_shape=jax.ShapeDtypeStruct((2, PW, NX), bf16),
        in_specs=[vmem(), smem()],
        out_specs=vmem(),
        scratch_shapes=[
            pltpu.VMEM((NXL, NZC, BLOCK, HALF), bf16),
            pltpu.VMEM((NZC, BLOCK, HALF), bf16),
            pltpu.VMEM((NZC, BLOCK, HALF), bf16),
            pltpu.VMEM((NZC, BLOCK, HALF), bf16),
            pltpu.VMEM((NZC, BLOCK, HALF), bf16),
            pltpu.VMEM((ANGLES, BLOCK, NX), bf16),
            pltpu.VMEM((NXL, NZC, BLOCK, CHUNK), bf16),
            dma(NXL, NZC), dma(NXL, NZC),
            dma(NZC), dma(NZC), dma(NZC), dma(NZC),
            dma(NXH, NY), dma(NXH, NY), dma(NXH, NY), dma(NXH, NY),
            dma(NXL, NZC), dma(NXL, NZC),
            dma(NZC), dma(NZC), dma(NZC), dma(NZC), dma(NZC), dma(NZC),
        ],
        compiler_params=pltpu.CompilerParams(collective_id=1, has_side_effects=True, vmem_limit_bytes=VMEM),
        name="volume_gradient",
    )(part, offs)


def per_device(volume, consensus, probe, intensities, positions, offsets):
    pos_count = positions.shape[1]
    forward, inverse = dft_tables()
    lines = volume.reshape(2 * PW, NX)
    off = jnp.broadcast_to(offsets, (8, LANES))
    measured = intensities.reshape(PW, pos_count * PW)
    proj, offs = project(lines, off)
    part = waves(proj, probe, measured, positions.reshape(-1), jnp.asarray(forward), jnp.asarray(inverse))
    grad = volume_gradient(part, offs.reshape(ANGLES * NXL * NZC, LANES))
    rate = math.sqrt(NX / (pos_count * lax.axis_size("slab") * ANGLES * PW))
    current = volume.astype(jnp.float32)
    step = grad[:, None].astype(jnp.float32)
    return current - rate * step - MIX * (current - consensus.astype(jnp.float32))


def solution(mesh):
    return jax.shard_map(
        per_device,
        mesh=mesh,
        in_specs=(
            P(None, "slab", None, None),
            P(None, "slab", None, None),
            P(),
            P("angle", None, "slab", None),
            P("angle", "slab"),
            P("angle", "slab"),
        ),
        out_specs=P(None, "slab", None, None),
        check_vma=False,
    )
```

time: 614 us -> 126 us (0.21)
  waiting for transfers between devices: 357 us -> 0 us
  blocking collectives: 130 us -> 0 us
  Pallas kernels: 0 us -> 121 us
  between operations: 45 us -> 0.81 us
  local copies, waits for them, and re-layouts: 43.8 us -> 2.43 us
  other arithmetic: 28.8 us -> 1.88 us
    psum x2 -> x0, waiting for transfers between devices: 323 us -> none  [the longest x1 230 us: per_device(): detector_grad = lax.psum(jnp.stack(grads_all, axis=1), 'slab')]
    unnamed x1 -> x0, blocking collectives: 130 us -> none
    pallas_call x0 -> x3, Pallas kernels: none -> 121 us  [the longest x1 55.4 us: project(): pl.pallas_call(project_kernel, out_shape=(jax.ShapeDtypeStruct((2 * PW, N...]
    all_gather x1 -> x0, waiting for transfers between devices: 34.2 us -> none  [per_device(): projection = lax.all_gather(summed, 'slab', axis=3, tiled=True)]
    dynamic_update_slice x16 -> x0, local copies, waits for them, and re-layouts: 32.6 us -> none  [per_device(): lax.dynamic_update_slice_in_dim(total, window + grads[:, :, item], starts...]
    add x15 -> x0, other arithmetic: 15.7 us -> none  [per_device(): window + grads[:, :, item]]
    dynamic_slice x18 -> x0, local copies, waits for them, and re-layouts: 7.11 us -> none  [the longest x17 4.26 us: per_device(): lax.dynamic_slice_in_dim(proj_now, starts[item], patch_width, 2)]
  transfers between devices with their start and end apart: 3 -> 0, of which waited for: 3 -> 0; matrix products, arithmetic and copies ran while one was open for 0% -> 0% of each run, Pallas kernels for 0% -> 0%
where the time goes in v1:
time: 126 us
  Pallas kernels  121 us (96%)
  local copies, waits for them, and re-layouts  2.43 us (2%)
  other arithmetic  1.88 us (1%)
    pallas_call x1, Pallas kernels, project(): pl.pallas_call(project_kernel, out_shape=(jax.ShapeDtypeStruct((2 * PW, N...  55.4 us
    pallas_call x1, Pallas kernels, volume_gradient(): pl.pallas_call(volume_kernel, out_shape=jax.ShapeDtypeStruct((2, PW, NX),...  55.3 us
    pallas_call x1, Pallas kernels, waves(): pl.pallas_call(wave_kernel, out_shape=jax.ShapeDtypeStruct((2 * PW, NX),...  9.91 us

profile of v1, /device:TPU:1, one launch (start us, length us, event | category | flops | bytes accessed | tf_op | source)
XLA Modules:
  0.0 125.7 jit_solution(6450486816661811048)
XLA Ops:
  0.0 0.0 copy-start.2
  0.0 0.0 copy-start.3
  0.0 0.0 copy-start.5
  0.0 0.0 copy-start.4
  0.7 1.2 copy.14
  1.9 0.0 copy-start
  1.9 1.2 copy-done
  3.1 55.4 %project.1 = (bf16[256,2048]{1,0:T(8,128)(2,1)S(1)}, s32[8,16,128]{2,1,0:T(8,128)S(1)}) custom-call(bf16[256,2048]{1,0:T(8,128)(2,1)S(1)} %bitcast.18, s32[8,128]{1,0:T(8,128)S(1)} %broadcast_in_dim.9.off), custom_call_target="tpu_custom_call" | custom-call | tf_op jit(solution)/shard_map/project/pallas_call | solution.py:456
  58.5 0.0 copy-done.2
  58.5 0.0 copy-done.3
  58.5 0.0 copy-done.5
  58.5 0.0 copy-done.4
  58.5 0.0 copy-start.1
  58.6 0.0 copy-start.6
  58.6 9.9 %waves.1.part = bf16[256,2048]{1,0:T(8,128)(2,1)S(1)} custom-call(bf16[256,2048]{1,0:T(8,128)(2,1)S(1)} %get-tuple-element.7.proj, bf16[2,128,128]{2,1,0:T(8,128)(2,1)S(1)} %copy-done.4, bf16[128,2048]{1,0:T(8,128)(2,1)S(1)} %bitcast.19, s32[16]{0:T(128)S(1)} %bitcast.21, bf16[256,256]{1,0:T(8,128)(2,1)S(1)} %copy-done.3, bf16[256,256]{1,0:T(8,128)(2,1)S(1)} %copy-done.2), custom_call_target="tpu_custom_call" | custom-call | tf_op jit(solution)/shard_map/waves/pallas_call | solution.py:485
  68.5 55.3 %volume_gradient.1 = bf16[2,128,2048]{2,1,0:T(8,128)(2,1)S(1)} custom-call(bf16[256,2048]{1,0:T(8,128)(2,1)S(1)} %waves.1.part, s32[128,128]{1,0:T(8,128)S(1)} %bitcast.20), custom_call_target="tpu_custom_call" | custom-call | tf_op jit(solution)/shard_map/volume_gradient/pallas_call | solution.py:498
  123.8 0.0 copy-done.1
  123.8 0.0 copy-done.6
  123.8 1.9 %fusion.1 = f32[2,1,128,2048]{3,2,1,0:T(8,128)} fusion(bf16[2,128,2048]{2,1,0:T(8,128)(2,1)S(1)} %volume_gradient.1, bf16[2,1,128,2048]{3,2,1,0:T(8,128)(2,1)S(1)} %copy-done.6, bf16[2,1,128,2048]{3,2,1,0:T(8,128)(2,1)S(1)} %copy-done.1), kind=kLoop, calls=%fused_computation.3 | loop fusion | flops 4194304 | bytes 5242880 | tf_op jit(solution)/shard_map/sub | solution.py:534
  (1 shorter events, 0.0 us)
Async XLA Ops:
  0.0 58.5 %copy-start.2 = (bf16[256,256]{1,0:T(8,128)(2,1)S(1)}, bf16[256,256]{1,0:T(8,128)(2,1)}, u32[]{:S(2)}) copy-start(bf16[256,256]{1,0:T(8,128)(2,1)} %constant.9.clone.inverse) | copy-start | bytes 393220
  0.0 58.5 %copy-start.3 = (bf16[256,256]{1,0:T(8,128)(2,1)S(1)}, bf16[256,256]{1,0:T(8,128)(2,1)}, u32[]{:S(2)}) copy-start(bf16[256,256]{1,0:T(8,128)(2,1)} %constant.8.clone.forward) | copy-start | bytes 393220
  0.0 58.5 %copy-start.5 = (s32[1,16]{1,0:T(1,128)S(1)}, s32[1,16]{1,0:T(1,128)}, u32[]{:S(2)}) copy-start(s32[1,16]{1,0:T(1,128)} %param.12) | copy-start | bytes 196
  0.0 58.5 %copy-start.4 = (bf16[2,128,128]{2,1,0:T(8,128)(2,1)S(1)}, bf16[2,128,128]{2,1,0:T(8,128)(2,1)}, u32[]{:S(2)}) copy-start(bf16[2,128,128]{2,1,0:T(8,128)(2,1)} %probe.1) | copy-start | bytes 196612
  1.9 1.2 copy-start
  58.5 65.3 %copy-start.1 = (bf16[2,1,128,2048]{3,2,1,0:T(8,128)(2,1)S(1)}, bf16[2,1,128,2048]{3,2,1,0:T(8,128)(2,1)}, u32[]{:S(2)}) copy-start(bf16[2,1,128,2048]{3,2,1,0:T(8,128)(2,1)} %param.8) | copy-start | bytes 3145732
  58.6 65.3 %copy-start.6 = (bf16[2,1,128,2048]{3,2,1,0:T(8,128)(2,1)S(1)}, bf16[2,1,128,2048]{3,2,1,0:T(8,128)(2,1)}, u32[]{:S(2)}) copy-start(bf16[2,1,128,2048]{3,2,1,0:T(8,128)(2,1)} %param.9) | copy-start | bytes 3145732

commit v2 on v1

v2 whole, which is shorter than its diff:
```python
import math

import jax
import jax.numpy as jnp
import ml_dtypes
import numpy as np
from jax import lax
from jax.experimental import pallas as pl
from jax.experimental.pallas import tpu as pltpu
from jax.sharding import PartitionSpec as P

MIX = 0.5
NX = 2048
PW = 128
LANES = 128
TILES = NX // LANES
NZC = 8
NXL = 2
NXH = 2
NY = 4
ANGLES = NXH * NY
BLOCK = 16
HALF = NX // 2
CHUNK = NX // NY
FAR_FIRST = (4, 3, 5, 2, 6, 1, 7, 0)
VMEM = 16 * 1024 * 1024


def dft_tables():
    indices = np.arange(PW, dtype=np.int64)
    phases = (indices[:, None] * indices[None, :] % PW).astype(np.float64) * (2.0 * math.pi / PW)
    factor = 1.0 / math.sqrt(PW)
    re = (np.cos(phases) * factor).astype(ml_dtypes.bfloat16)
    im = (-np.sin(phases) * factor).astype(ml_dtypes.bfloat16)
    forward = np.block([[re, im], [-im, re]])
    inverse = np.block([[re, -im], [im, re]])
    return forward.astype(ml_dtypes.bfloat16), inverse.astype(ml_dtypes.bfloat16)


class Here:
    def __init__(self):
        s = lax.axis_index("slab")
        a = lax.axis_index("angle")
        self.a = a
        self.c = lax.rem(s, 2)
        self.xl = lax.rem(lax.div(s, 2), 2)
        self.zc = lax.div(s, 4)
        self.y = lax.rem(a, NY)
        self.xh = lax.div(a, NY)
        self.m = self.xl * NZC + self.zc

    def z_of(self, rel):
        return lax.rem(self.zc + rel, NZC)

    def y_of(self, rel):
        return lax.rem(self.y + rel, NY)

    def x_of(self, flip):
        return 1 - self.xl if flip else self.xl

    def chip(self, rel_z, flip_x):
        return self.device(zc=self.z_of(rel_z), xl=self.x_of(flip_x))

    def angle_peer(self, flip_xh, rel_y):
        return self.device(xh=1 - self.xh if flip_xh else self.xh, y=self.y_of(rel_y))

    def device(self, zc=None, xl=None, c=None, xh=None, y=None):
        zc = self.zc if zc is None else zc
        xl = self.xl if xl is None else xl
        c = self.c if c is None else c
        xh = self.xh if xh is None else xh
        y = self.y if y is None else y
        return {"slab": zc * 4 + xl * 2 + c, "angle": xh * NY + y}

    @property
    def sibling(self):
        return self.device(c=1 - self.c)

    def greet(self):
        peers = [self.sibling]
        peers += [self.chip(r, f) for f in (0, 1) for r in range(NZC) if r or f]
        peers += [self.angle_peer(f, r) for f in (0, 1) for r in range(NY) if r or f]
        barrier = pltpu.get_barrier_semaphore()
        for peer in peers:
            pl.semaphore_signal(barrier, 1, device_id=peer, device_id_type=pl.DeviceIdType.MESH)
        pl.semaphore_wait(barrier, len(peers))


def rows16(block):
    return pl.ds(pl.multiple_of(block * BLOCK, BLOCK), BLOCK)


def half_cols(core):
    return pl.ds(pl.multiple_of(core * HALF, HALF), HALF)


def chunk_cols(y):
    return pl.ds(pl.multiple_of(y * CHUNK, CHUNK), CHUNK)


def remote(src, dst, send, recv, to):
    return pltpu.make_async_remote_copy(
        src_ref=src,
        dst_ref=dst,
        send_sem=send,
        recv_sem=recv,
        device_id=to,
        device_id_type=pl.DeviceIdType.MESH,
    )


def shifted_tiles(tiles, start, count):
    first = lax.div(start, LANES)
    inner = lax.rem(start, LANES)
    need = min(count + 1, TILES)
    for stride in (8, 4, 2, 1):
        keep = min(need + stride - 1, TILES)
        bit = lax.rem(lax.div(first, stride), 2) == 1
        size = len(tiles)
        tiles = [lax.select_n(bit, tiles[j], tiles[(j + stride) % size]) for j in range(keep)]
    back = lax.rem(LANES - inner, LANES)
    lane = lax.broadcasted_iota(jnp.int32, (BLOCK, LANES), 1)
    stay = lane < LANES - inner
    turned = [pltpu.roll(tile.astype(jnp.float32), back, 1) for tile in tiles]
    return [jnp.where(stay, turned[j], turned[(j + 1) % need]) for j in range(count)]


def tiles_of(row):
    return [row[:, j * LANES : (j + 1) * LANES] for j in range(TILES)]


class Copies:
    def __init__(self, here):
        self.here = here
        self.sent = []

    def start(self, src, dst, send, recv, to):
        copy = remote(src, dst, send, recv, to)
        copy.start()
        self.sent.append(copy)

    def arrived(self, ref, recv):
        remote(ref, ref, recv, recv, self.here.sibling).wait_recv()

    def drain(self):
        for copy in self.sent:
            copy.wait_send()


def to_y(here, copies, piece, k, sems):
    send, recv = sems
    mine = piece(here.y)
    for d in (1, 3, 2):
        copies.start(mine, mine, send.at[d, k], recv.at[NY - d, k], here.angle_peer(0, d))


def from_y(here, copies, piece, k, sems):
    send, recv = sems
    for d in (1, 3, 2):
        copies.arrived(piece(here.y_of(d)), recv.at[d, k])


def project_kernel(
    vol, off, proj, offs_out, gath, acc, sib, offt, offv, offs_s,
    s_off, r_off, s_t1, r_t1, s_y, r_y, s_sib, r_sib, s_z, r_z, s_x, r_x, s_c, r_c, s_oa, r_oa, l_sem,
):
    here = Here()
    offt[here.m] = jnp.full((8, LANES), off[0, 0], jnp.int32)
    here.greet()
    copies = Copies(here)
    order = (0, 1, 7, 2, 6, 3, 5, 4)
    cols = chunk_cols(here.y)
    for rel in order:
        r = (NZC - rel) % NZC
        for f in (0, 1):
            if rel or f:
                to = here.chip(r, f)
                block = here.x_of(f) * NZC + here.z_of(r)
                copies.start(offt.at[here.m], offt.at[here.m], s_off.at[f, rel], r_off.at[f, rel], to)
                copies.start(
                    vol.at[rows16(block), cols], gath.at[f, rel, :, cols], s_t1.at[f, rel], r_t1.at[f, rel], to
                )
    own = pltpu.make_async_copy(vol.at[rows16(here.m)], gath.at[0, 0], l_sem.at[0])
    own.start()

    def piece(rel):
        if rel == 0:
            return lambda y: gath.at[1, 0, :, chunk_cols(y)]
        return lambda y: gath.at[:, rel, :, chunk_cols(y)]

    for rel in order:
        for f in (0, 1):
            if rel or f:
                copies.arrived(gath.at[f, rel, :, cols], r_t1.at[f, rel])
        to_y(here, copies, piece(rel), rel, (s_y, r_y))

    for f in (0, 1):
        for r in range(NZC):
            if r or f:
                copies.arrived(offt.at[here.x_of(f) * NZC + here.z_of(r)], r_off.at[f, r])
    for g in range(NXL * NZC):
        offv[g : g + 1, :] = offt[g, 0:1, :]
    down = pltpu.make_async_copy(offv, offs_s, l_sem.at[1])
    down.start()
    for f in (0, 1):
        for r in range(NY):
            if r or f:
                back = (NY - r) % NY
                copies.start(offv, offs_out.at[here.a], s_oa.at[f, r], r_oa.at[f, back], here.angle_peer(f, r))
    offs_out[here.a] = offv[...]
    down.wait()
    own.wait()
    acc[...] = jnp.zeros_like(acc)
    for rel in order:
        from_y(here, copies, piece(rel), rel, (s_y, r_y))

        def add_slot(f, carry):
            g = lax.rem(here.xl + f, NXL) * NZC + here.z_of(rel)
            for j, tile in enumerate(shifted_tiles(tiles_of(gath[f, rel]), offs_s[g, 0], TILES)):
                acc[:, j * LANES : (j + 1) * LANES] += tile
            return carry

        lax.fori_loop(0, NXL, add_slot, 0)

    mine, other = half_cols(here.c), half_cols(1 - here.c)
    copies.start(acc.at[:, other], sib, s_sib, r_sib, here.sibling)
    copies.arrived(sib, r_sib)
    proj[rows16(here.m), mine] = (acc[:, mine] + sib[...]).astype(jnp.bfloat16)

    own = proj.at[rows16(here.m), mine]
    for r in (1, 7, 2, 6, 3, 5, 4):
        copies.start(own, own, s_z.at[r], r_z.at[(NZC - r) % NZC], here.chip(r, 0))
    copies.start(own, own, s_x.at[0], r_x.at[0], here.chip(0, 1))
    copies.start(own, own, s_c.at[0, 0], r_c.at[0, 0], here.sibling)
    for rel in (1, 7, 2, 6, 3, 5, 4):
        got = proj.at[rows16(here.xl * NZC + here.z_of(rel)), mine]
        copies.arrived(got, r_z.at[rel])
        copies.start(got, got, s_x.at[rel], r_x.at[rel], here.chip(0, 1))
        copies.start(got, got, s_c.at[0, rel], r_c.at[0, rel], here.sibling)
    for rel in order:
        got = proj.at[rows16(here.x_of(1) * NZC + here.z_of(rel)), mine]
        copies.arrived(got, r_x.at[rel])
        copies.start(got, got, s_c.at[1, rel], r_c.at[1, rel], here.sibling)
    for f in (0, 1):
        for rel in order:
            copies.arrived(proj.at[rows16(here.x_of(f) * NZC + here.z_of(rel)), other], r_c.at[f, rel])
    for f in (0, 1):
        for r in range(NY):
            if r or f:
                a_from = (1 - here.xh if f else here.xh) * NY + here.y_of(r)
                copies.arrived(offs_out.at[a_from], r_oa.at[f, r])
    copies.drain()


GROUP = 8


def wave_kernel(proj, probe, measured, pos, forward, inverse, out, total):
    total[...] = jnp.zeros_like(total)
    count = measured.shape[1] // PW

    def swap(x):
        n = x.shape[0] // PW
        parts = [[x[k * PW : (k + 1) * PW, h * PW : (h + 1) * PW] for k in range(n)] for h in range(2)]
        return jnp.concatenate([jnp.concatenate(p, axis=1) for p in parts], axis=0)

    def one_group(group, carry):
        p_re = probe[0].astype(jnp.float32)
        p_im = probe[1].astype(jnp.float32)
        fwd = forward[...]
        inv = inverse[...]
        starts = []
        exits = []
        for k in range(GROUP):
            at = pos[GROUP * group + k]
            first = jnp.minimum(lax.div(at, LANES), TILES - 2)
            inner = at - first * LANES
            where = pl.ds(pl.multiple_of(first * LANES, LANES), 2 * LANES)
            starts.append((where, inner))
            row = lax.broadcasted_iota(jnp.int32, (2 * LANES, PW), 0)
            col = lax.broadcasted_iota(jnp.int32, (2 * LANES, PW), 1)
            pick = jnp.where(row == col + inner, 1.0, 0.0).astype(jnp.bfloat16)
            patch = jnp.dot(proj[:, where], pick, preferred_element_type=jnp.float32)
            re, im = patch[:PW], patch[PW:]
            exits.append(
                jnp.concatenate([p_re * re - p_im * im, p_re * im + p_im * re], axis=1).astype(jnp.bfloat16)
            )
        half = jnp.dot(jnp.concatenate(exits, axis=0), fwd, preferred_element_type=jnp.float32).astype(jnp.bfloat16)
        far = jnp.dot(inv, swap(half), preferred_element_type=jnp.float32)
        waves = []
        for k in range(GROUP):
            f_re = far[:PW, k * PW : (k + 1) * PW]
            f_im = far[PW:, k * PW : (k + 1) * PW]
            at = pl.multiple_of((GROUP * group + k) * PW, PW)
            target = measured[:, pl.ds(at, PW)].astype(jnp.float32)
            misfit = f_re * f_re + f_im * f_im - target
            waves.append(jnp.concatenate([misfit * f_re, misfit * f_im], axis=1).astype(jnp.bfloat16))
        back = jnp.dot(jnp.concatenate(waves, axis=0), inv, preferred_element_type=jnp.float32).astype(jnp.bfloat16)
        grad = jnp.dot(fwd, swap(back), preferred_element_type=jnp.float32)
        placed = []
        for k, (where, inner) in enumerate(starts):
            g_re = grad[:PW, k * PW : (k + 1) * PW]
            g_im = grad[PW:, k * PW : (k + 1) * PW]
            patch_grad = jnp.concatenate(
                [p_re * g_re + p_im * g_im, p_re * g_im - p_im * g_re], axis=0
            ).astype(jnp.bfloat16)
            row = lax.broadcasted_iota(jnp.int32, (PW, 2 * LANES), 0)
            col = lax.broadcasted_iota(jnp.int32, (PW, 2 * LANES), 1)
            put = jnp.where(col == row + inner, 1.0, 0.0).astype(jnp.bfloat16)
            placed.append(jnp.dot(patch_grad, put, preferred_element_type=jnp.float32))
        for (where, inner), value in zip(starts, placed):
            total[:, where] += value
        return carry

    lax.fori_loop(0, count // GROUP, one_group, 0)
    out[...] = total[...].astype(jnp.bfloat16)


def volume_kernel(
    part, offs, out, cbuf, xsend, xbuf, zsend, zbuf, dgall, vsend,
    s_c, r_c, s_x, r_x, s_z, r_z, s_a, r_a, s_s, r_s, s_v, r_v, s_y, r_y,
):
    here = Here()
    here.greet()
    copies = Copies(here)
    mine, other = half_cols(here.c), half_cols(1 - here.c)
    for f in (1, 0):
        for r in FAR_FIRST:
            src = part.at[rows16(here.x_of(f) * NZC + here.z_of(r)), other]
            copies.start(src, cbuf.at[f, r], s_c.at[f, r], r_c.at[f, r], here.sibling)
    for r in FAR_FIRST:
        copies.arrived(cbuf.at[1, r], r_c.at[1, r])
        own = part[rows16(here.x_of(1) * NZC + here.z_of(r)), mine]
        xsend[r] = (own.astype(jnp.float32) + cbuf[1, r].astype(jnp.float32)).astype(jnp.bfloat16)
        copies.start(xsend.at[r], xbuf.at[r], s_x.at[r], r_x.at[r], here.chip(0, 1))
    total = None
    for r in FAR_FIRST:
        copies.arrived(cbuf.at[0, r], r_c.at[0, r])
        own = part[rows16(here.xl * NZC + here.z_of(r)), mine]
        value = own.astype(jnp.float32) + cbuf[0, r].astype(jnp.float32)
        copies.arrived(xbuf.at[r], r_x.at[r])
        value = value + xbuf[r].astype(jnp.float32)
        if r:
            zsend[r] = value.astype(jnp.bfloat16)
            slot = (NZC - r) % NZC
            copies.start(zsend.at[r], zbuf.at[slot], s_z.at[r], r_z.at[slot], here.chip(r, 0))
        else:
            total = value
    for r in (1, 7, 2, 6, 3, 5, 4):
        copies.arrived(zbuf.at[r], r_z.at[r])
        total = total + zbuf[r].astype(jnp.float32)
    dgall[here.a, :, mine] = total.astype(jnp.bfloat16)
    own = dgall.at[here.a, :, mine]
    peers = [(0, 1), (0, 3), (1, 0), (0, 2), (1, 1), (1, 3), (1, 2)]
    for f, r in peers:
        copies.start(own, own, s_a.at[f, r], r_a.at[f, (NY - r) % NY], here.angle_peer(f, r))
    copies.start(own, own, s_s.at[0, 0], r_s.at[0, 0], here.sibling)

    def angle_of(f, r):
        return (1 - here.xh if f else here.xh) * NY + here.y_of(r)

    for f, r in peers:
        got = dgall.at[angle_of(f, r), :, mine]
        copies.arrived(got, r_a.at[f, r])
        copies.start(got, got, s_s.at[f, r], r_s.at[f, r], here.sibling)
    for f, r in [(0, 0)] + peers:
        copies.arrived(dgall.at[angle_of(f, r), :, other], r_s.at[f, r])

    cols = chunk_cols(here.y)
    zrows = rows16(here.zc)

    def gradient(f, r):
        g = here.x_of(f) * NZC + here.z_of(r)

        def add_angle(b, sums):
            first = lax.rem(here.y * CHUNK + NX - offs[b * NXL * NZC + g, 0], NX)
            tiles = shifted_tiles(tiles_of(dgall[b]), first, CHUNK // LANES)
            return [x + t for x, t in zip(sums, tiles)]

        sums = [jnp.zeros((BLOCK, LANES), jnp.float32)] * (CHUNK // LANES)
        sums = lax.fori_loop(0, ANGLES, add_angle, sums, unroll=2)
        return jnp.concatenate(sums, axis=1).astype(jnp.bfloat16)

    for r in FAR_FIRST:
        for f in (1, 0):
            value = gradient(f, r)
            if r or f:
                slot = (NZC - r) % NZC
                vsend[f, r] = value
                copies.start(
                    vsend.at[f, r], out.at[here.xl, zrows, cols], s_v.at[f, r], r_v.at[f, slot], here.chip(r, f)
                )
            else:
                out[here.xl, zrows, cols] = value

    def piece(rel):
        return lambda y: out.at[:, rows16(here.z_of(rel)), chunk_cols(y)]

    order = (0, 1, 7, 2, 6, 3, 5, 4)
    for rel in order:
        for f in (0, 1):
            if rel or f:
                copies.arrived(out.at[here.x_of(f), rows16(here.z_of(rel)), cols], r_v.at[f, rel])
        to_y(here, copies, piece(rel), rel, (s_y, r_y))
    for rel in order:
        from_y(here, copies, piece(rel), rel, (s_y, r_y))
    copies.drain()


def dma(*shape):
    return pltpu.SemaphoreType.DMA(shape)


def vmem():
    return pl.BlockSpec(memory_space=pltpu.VMEM)


def smem():
    return pl.BlockSpec(memory_space=pltpu.SMEM)


def project(lines, off):
    return pl.pallas_call(
        project_kernel,
        out_shape=(
            jax.ShapeDtypeStruct((2 * PW, NX), jnp.bfloat16),
            jax.ShapeDtypeStruct((ANGLES, NXL * NZC, LANES), jnp.int32),
        ),
        in_specs=[vmem(), smem()],
        out_specs=(vmem(), vmem()),
        scratch_shapes=[
            pltpu.VMEM((NXL, NZC, BLOCK, NX), jnp.bfloat16),
            pltpu.VMEM((BLOCK, NX), jnp.float32),
            pltpu.VMEM((BLOCK, HALF), jnp.float32),
            pltpu.VMEM((NXL * NZC, 8, LANES), jnp.int32),
            pltpu.VMEM((NXL * NZC, LANES), jnp.int32),
            pltpu.SMEM((NXL * NZC, LANES), jnp.int32),
            dma(NXL, NZC), dma(NXL, NZC), dma(NXL, NZC), dma(NXL, NZC),
            dma(NY, NZC), dma(NY, NZC),
            pltpu.SemaphoreType.DMA, pltpu.SemaphoreType.DMA,
            dma(NZC), dma(NZC), dma(NZC), dma(NZC),
            dma(NXL, NZC), dma(NXL, NZC),
            dma(NXH, NY), dma(NXH, NY),
            dma(2),
        ],
        compiler_params=pltpu.CompilerParams(collective_id=0, has_side_effects=True, vmem_limit_bytes=VMEM),
        name="project",
    )(lines, off)


def waves(proj, probe, measured, pos, forward, inverse):
    return pl.pallas_call(
        wave_kernel,
        out_shape=jax.ShapeDtypeStruct((2 * PW, NX), jnp.bfloat16),
        in_specs=[vmem(), vmem(), vmem(), smem(), vmem(), vmem()],
        out_specs=vmem(),
        scratch_shapes=[pltpu.VMEM((2 * PW, NX), jnp.float32)],
        compiler_params=pltpu.CompilerParams(vmem_limit_bytes=2 * VMEM),
        name="waves",
    )(proj, probe, measured, pos, forward, inverse)


def volume_gradient(part, offs):
    bf16 = jnp.bfloat16
    return pl.pallas_call(
        volume_kernel,
        out_shape=jax.ShapeDtypeStruct((2, PW, NX), bf16),
        in_specs=[vmem(), smem()],
        out_specs=vmem(),
        scratch_shapes=[
            pltpu.VMEM((NXL, NZC, BLOCK, HALF), bf16),
            pltpu.VMEM((NZC, BLOCK, HALF), bf16),
            pltpu.VMEM((NZC, BLOCK, HALF), bf16),
            pltpu.VMEM((NZC, BLOCK, HALF), bf16),
            pltpu.VMEM((NZC, BLOCK, HALF), bf16),
            pltpu.VMEM((ANGLES, BLOCK, NX), bf16),
            pltpu.VMEM((NXL, NZC, BLOCK, CHUNK), bf16),
            dma(NXL, NZC), dma(NXL, NZC),
            dma(NZC), dma(NZC), dma(NZC), dma(NZC),
            dma(NXH, NY), dma(NXH, NY), dma(NXH, NY), dma(NXH, NY),
            dma(NXL, NZC), dma(NXL, NZC),
            dma(NY, NZC), dma(NY, NZC),
        ],
        compiler_params=pltpu.CompilerParams(collective_id=1, has_side_effects=True, vmem_limit_bytes=VMEM),
        name="volume_gradient",
    )(part, offs)


def per_device(volume, consensus, probe, intensities, positions, offsets):
    pos_count = positions.shape[1]
    forward, inverse = dft_tables()
    lines = volume.reshape(2 * PW, NX)
    measured = intensities.reshape(PW, pos_count * PW)
    proj, offs = project(lines, offsets)
    part = waves(proj, probe, measured, positions.reshape(-1), jnp.asarray(forward), jnp.asarray(inverse))
    grad = volume_gradient(part, offs.reshape(ANGLES * NXL * NZC, LANES))
    rate = math.sqrt(NX / (pos_count * lax.axis_size("slab") * ANGLES * PW))
    current = volume.astype(jnp.float32)
    step = grad[:, None].astype(jnp.float32)
    return current - rate * step - MIX * (current - consensus.astype(jnp.float32))


def solution(mesh):
    return jax.shard_map(
        per_device,
        mesh=mesh,
        in_specs=(
            P(None, "slab", None, None),
            P(None, "slab", None, None),
            P(),
            P("angle", None, "slab", None),
            P("angle", "slab"),
            P("angle", "slab"),
        ),
        out_specs=P(None, "slab", None, None),
        check_vma=False,
    )
```

time: 126 us -> 101 us (0.80)
  Pallas kernels: 121 us -> 95.7 us
    pallas_call x1, Pallas kernels: 55.4 us -> 41.4 us  [project(): pl.pallas_call(project_kernel, out_shape=(jax.ShapeDtypeStruct((2 * PW, N...]
    pallas_call x1, Pallas kernels: 9.91 us -> 4.01 us  [waves(): pl.pallas_call(wave_kernel, out_shape=jax.ShapeDtypeStruct((2 * PW, NX),...]
    pallas_call x1, Pallas kernels: 55.3 us -> 50.2 us  [volume_gradient(): pl.pallas_call(volume_kernel, out_shape=jax.ShapeDtypeStruct((2, PW, NX),...]
where the time goes in v2:
time: 101 us
  Pallas kernels  95.7 us (95%)
  local copies, waits for them, and re-layouts  2.43 us (2%)
  other arithmetic  1.88 us (2%)
    pallas_call x1, Pallas kernels, volume_gradient(): pl.pallas_call(volume_kernel, out_shape=jax.ShapeDtypeStruct((2, PW, NX),...  50.2 us
    pallas_call x1, Pallas kernels, project(): pl.pallas_call(project_kernel, out_shape=(jax.ShapeDtypeStruct((2 * PW, N...  41.4 us
    pallas_call x1, Pallas kernels, waves(): pl.pallas_call(wave_kernel, out_shape=jax.ShapeDtypeStruct((2 * PW, NX),...  4.01 us
    unnamed x15, local copies, waits for them, and re-layouts  2.43 us

profile of v2, /device:TPU:1, one launch (start us, length us, event | category | flops | bytes accessed | tf_op | source)
XLA Modules:
  0.0 100.8 jit_solution(10325625260911104137)
XLA Ops:
  0.0 0.0 copy-start.2
  0.0 0.0 copy-start.3
  0.0 0.0 copy-start.5
  0.0 0.0 copy-start.4
  0.7 1.2 %copy.14 = bf16[16,8,16,128]{3,1,2,0:T(8,128)(2,1)S(1)} copy(bf16[16,8,16,128]{3,2,1,0:T(8,128)(2,1)} %bitcast.20) | data formatting | bytes 1048576
  1.9 0.0 copy-start
  1.9 1.2 %copy-done = bf16[2,1,128,2048]{3,2,1,0:T(8,128)(2,1)S(1)} copy-done((bf16[2,1,128,2048]{3,2,1,0:T(8,128)(2,1)S(1)}, bf16[2,1,128,2048]{3,2,1,0:T(8,128)(2,1)}, u32[]{:S(2)}) %copy-start) | copy-done | bytes 1048600
  3.1 41.4 %project.1 = (bf16[256,2048]{1,0:T(8,128)(2,1)S(1)}, s32[8,16,128]{2,1,0:T(8,128)S(1)}) custom-call(bf16[256,2048]{1,0:T(8,128)(2,1)S(1)} %bitcast.16, s32[1,1]{1,0:T(1,128)S(6)} %copy.15.off), custom_call_target="tpu_custom_call" | custom-call | tf_op jit(solution)/shard_map/project/pallas_call | solution.py:423
  44.5 0.0 copy-done.2
  44.5 0.0 copy-done.3
  44.5 0.0 copy-done.5
  44.6 0.0 copy-done.4
  44.6 0.0 copy-start.1
  44.6 0.0 copy-start.6
  44.6 4.0 %waves.1.part = bf16[256,2048]{1,0:T(8,128)(2,1)S(1)} custom-call(bf16[256,2048]{1,0:T(8,128)(2,1)S(1)} %get-tuple-element.7.proj, bf16[2,128,128]{2,1,0:T(8,128)(2,1)S(1)} %copy-done.4, bf16[128,2048]{1,0:T(8,128)(2,1)S(1)} %bitcast.17, s32[16]{0:T(128)S(1)} %bitcast.19, bf16[256,256]{1,0:T(8,128)(2,1)S(1)} %copy-done.3, bf16[256,256]{1,0:T(8,128)(2,1)S(1)} %copy-done.2), custom_call_target="tpu_custom_call" | custom-call | tf_op jit(solution)/shard_map/waves/pallas_call | solution.py:452
  48.6 50.2 %volume_gradient.1 = bf16[2,128,2048]{2,1,0:T(8,128)(2,1)S(1)} custom-call(bf16[256,2048]{1,0:T(8,128)(2,1)S(1)} %waves.1.part, s32[128,128]{1,0:T(8,128)S(1)} %bitcast.18), custom_call_target="tpu_custom_call" | custom-call | tf_op jit(solution)/shard_map/volume_gradient/pallas_call | solution.py:465
  98.9 0.0 copy-done.1
  98.9 0.0 copy-done.6
  98.9 1.9 %fusion.1 = f32[2,1,128,2048]{3,2,1,0:T(8,128)} fusion(bf16[2,128,2048]{2,1,0:T(8,128)(2,1)S(1)} %volume_gradient.1, bf16[2,1,128,2048]{3,2,1,0:T(8,128)(2,1)S(1)} %copy-done.6, bf16[2,1,128,2048]{3,2,1,0:T(8,128)(2,1)S(1)} %copy-done.1), kind=kLoop, calls=%fused_computation.3 | loop fusion | flops 4194304 | bytes 5242880 | tf_op jit(solution)/shard_map/sub | solution.py:500
Async XLA Ops:
  0.0 44.5 %copy-start.2 = (bf16[256,256]{1,0:T(8,128)(2,1)S(1)}, bf16[256,256]{1,0:T(8,128)(2,1)}, u32[]{:S(2)}) copy-start(bf16[256,256]{1,0:T(8,128)(2,1)} %constant.9.clone.inverse) | copy-start | bytes 393220
  0.0 44.5 %copy-start.3 = (bf16[256,256]{1,0:T(8,128)(2,1)S(1)}, bf16[256,256]{1,0:T(8,128)(2,1)}, u32[]{:S(2)}) copy-start(bf16[256,256]{1,0:T(8,128)(2,1)} %constant.8.clone.forward) | copy-start | bytes 393220
  0.0 44.5 %copy-start.5 = (s32[1,16]{1,0:T(1,128)S(1)}, s32[1,16]{1,0:T(1,128)}, u32[]{:S(2)}) copy-start(s32[1,16]{1,0:T(1,128)} %param.12) | copy-start | bytes 196
  0.0 44.5 %copy-start.4 = (bf16[2,128,128]{2,1,0:T(8,128)(2,1)S(1)}, bf16[2,128,128]{2,1,0:T(8,128)(2,1)}, u32[]{:S(2)}) copy-start(bf16[2,128,128]{2,1,0:T(8,128)(2,1)} %probe.1) | copy-start | bytes 196612
  1.9 1.2 %copy-start = (bf16[2,1,128,2048]{3,2,1,0:T(8,128)(2,1)S(1)}, bf16[2,1,128,2048]{3,2,1,0:T(8,128)(2,1)}, u32[]{:S(2)}) copy-start(bf16[2,1,128,2048]{3,2,1,0:T(8,128)(2,1)} %param.8) | copy-start | bytes 3145732
  44.6 54.3 %copy-start.1 = (bf16[2,1,128,2048]{3,2,1,0:T(8,128)(2,1)S(1)}, bf16[2,1,128,2048]{3,2,1,0:T(8,128)(2,1)}, u32[]{:S(2)}) copy-start(bf16[2,1,128,2048]{3,2,1,0:T(8,128)(2,1)} %param.8) | copy-start | bytes 3145732
  44.6 54.3 %copy-start.6 = (bf16[2,1,128,2048]{3,2,1,0:T(8,128)(2,1)S(1)}, bf16[2,1,128,2048]{3,2,1,0:T(8,128)(2,1)}, u32[]{:S(2)}) copy-start(bf16[2,1,128,2048]{3,2,1,0:T(8,128)(2,1)} %param.9) | copy-start | bytes 3145732

commit v3 on v2

--- a/solution.py
+++ b/solution.py
@@ -110,15 +110,16 @@
 
 
 def shifted_tiles(tiles, start, count):
-    first = lax.div(start, LANES)
-    inner = lax.rem(start, LANES)
+    first = start >> 7
+    inner = start & (LANES - 1)
     need = min(count + 1, TILES)
-    for stride in (8, 4, 2, 1):
+    for level in (3, 2, 1, 0):
+        stride = 1 << level
         keep = min(need + stride - 1, TILES)
-        bit = lax.rem(lax.div(first, stride), 2) == 1
+        bit = (first >> level) & 1 == 1
         size = len(tiles)
         tiles = [lax.select_n(bit, tiles[j], tiles[(j + stride) % size]) for j in range(keep)]
-    back = lax.rem(LANES - inner, LANES)
+    back = (LANES - inner) & (LANES - 1)
     lane = lax.broadcasted_iota(jnp.int32, (BLOCK, LANES), 1)
     stay = lane < LANES - inner
     turned = [pltpu.roll(tile.astype(jnp.float32), back, 1) for tile in tiles]
@@ -371,32 +372,28 @@
 
     def gradient(f, r):
         g = here.x_of(f) * NZC + here.z_of(r)
-
-        def add_angle(b, sums):
-            first = lax.rem(here.y * CHUNK + NX - offs[b * NXL * NZC + g, 0], NX)
+        sums = None
+        for b in range(ANGLES):
+            first = (here.y * CHUNK + NX - offs[b * NXL * NZC + g, 0]) & (NX - 1)
             tiles = shifted_tiles(tiles_of(dgall[b]), first, CHUNK // LANES)
-            return [x + t for x, t in zip(sums, tiles)]
-
-        sums = [jnp.zeros((BLOCK, LANES), jnp.float32)] * (CHUNK // LANES)
-        sums = lax.fori_loop(0, ANGLES, add_angle, sums, unroll=2)
+            sums = tiles if sums is None else [x + t for x, t in zip(sums, tiles)]
         return jnp.concatenate(sums, axis=1).astype(jnp.bfloat16)
 
-    for r in FAR_FIRST:
-        for f in (1, 0):
-            value = gradient(f, r)
+    order = (0, 1, 7, 2, 6, 3, 5, 4)
+    for rel in order:
+        r = (NZC - rel) % NZC
+        for f in (0, 1):
             if r or f:
-                slot = (NZC - r) % NZC
-                vsend[f, r] = value
+                vsend[f, r] = gradient(f, r)
                 copies.start(
-                    vsend.at[f, r], out.at[here.xl, zrows, cols], s_v.at[f, r], r_v.at[f, slot], here.chip(r, f)
+                    vsend.at[f, r], out.at[here.xl, zrows, cols], s_v.at[f, r], r_v.at[f, rel], here.chip(r, f)
                 )
             else:
-                out[here.xl, zrows, cols] = value
+                out[here.xl, zrows, cols] = gradient(f, r)
 
     def piece(rel):
         return lambda y: out.at[:, rows16(here.z_of(rel)), chunk_cols(y)]
 
-    order = (0, 1, 7, 2, 6, 3, 5, 4)
     for rel in order:
         for f in (0, 1):
             if rel or f:

time: 101 us -> 95.1 us (0.942)
  Pallas kernels: 95.7 us -> 89.9 us
    pallas_call x1, Pallas kernels: 50.2 us -> 44.5 us  [volume_gradient(): pl.pallas_call(volume_kernel, out_shape=jax.ShapeDtypeStruct((2, PW, NX),...]
where the time goes in v3:
time: 95.1 us; the launch traced here: 95 us
  Pallas kernels  89.9 us (95%)
  local copies, waits for them, and re-layouts  2.43 us (3%)
  other arithmetic  1.88 us (2%)
    pallas_call x1, Pallas kernels, volume_gradient(): pl.pallas_call(volume_kernel, out_shape=jax.ShapeDtypeStruct((2, PW, NX),...  44.5 us
    pallas_call x1, Pallas kernels, project(): pl.pallas_call(project_kernel, out_shape=(jax.ShapeDtypeStruct((2 * PW, N...  41.4 us
    pallas_call x1, Pallas kernels, waves(): pl.pallas_call(wave_kernel, out_shape=jax.ShapeDtypeStruct((2 * PW, NX),...  4.01 us
    unnamed x15, local copies, waits for them, and re-layouts  2.43 us

profile of v3, /device:TPU:1, one launch (start us, length us, event | category | flops | bytes accessed | tf_op | source)
XLA Modules:
  0.0 95.0 jit_solution(8557978051976722911)
XLA Ops:
  0.0 0.0 copy-start.2
  0.0 0.0 copy-start.3
  0.0 0.0 copy-start.5
  0.0 0.0 copy-start.4
  0.7 1.2 %copy.14 = bf16[16,8,16,128]{3,1,2,0:T(8,128)(2,1)S(1)} copy(bf16[16,8,16,128]{3,2,1,0:T(8,128)(2,1)} %bitcast.20) | data formatting | bytes 1048576
  1.9 0.0 copy-start
  1.9 1.2 %copy-done = bf16[2,1,128,2048]{3,2,1,0:T(8,128)(2,1)S(1)} copy-done((bf16[2,1,128,2048]{3,2,1,0:T(8,128)(2,1)S(1)}, bf16[2,1,128,2048]{3,2,1,0:T(8,128)(2,1)}, u32[]{:S(2)}) %copy-start) | copy-done | bytes 1048600
  3.1 41.4 %project.1 = (bf16[256,2048]{1,0:T(8,128)(2,1)S(1)}, s32[8,16,128]{2,1,0:T(8,128)S(1)}) custom-call(bf16[256,2048]{1,0:T(8,128)(2,1)S(1)} %bitcast.16, s32[1,1]{1,0:T(1,128)S(6)} %copy.15.off), custom_call_target="tpu_custom_call" | custom-call | tf_op jit(solution)/shard_map/project/pallas_call | solution.py:420
  44.5 0.0 copy-done.2
  44.5 0.0 copy-done.3
  44.5 0.0 copy-done.5
  44.5 0.0 copy-done.4
  44.6 0.0 copy-start.1
  44.6 0.0 copy-start.6
  44.6 4.0 %waves.1.part = bf16[256,2048]{1,0:T(8,128)(2,1)S(1)} custom-call(bf16[256,2048]{1,0:T(8,128)(2,1)S(1)} %get-tuple-element.7.proj, bf16[2,128,128]{2,1,0:T(8,128)(2,1)S(1)} %copy-done.4, bf16[128,2048]{1,0:T(8,128)(2,1)S(1)} %bitcast.17, s32[16]{0:T(128)S(1)} %bitcast.19, bf16[256,256]{1,0:T(8,128)(2,1)S(1)} %copy-done.3, bf16[256,256]{1,0:T(8,128)(2,1)S(1)} %copy-done.2), custom_call_target="tpu_custom_call" | custom-call | tf_op jit(solution)/shard_map/waves/pallas_call | solution.py:449
  48.6 44.5 %volume_gradient.1 = bf16[2,128,2048]{2,1,0:T(8,128)(2,1)S(1)} custom-call(bf16[256,2048]{1,0:T(8,128)(2,1)S(1)} %waves.1.part, s32[128,128]{1,0:T(8,128)S(1)} %bitcast.18), custom_call_target="tpu_custom_call" | custom-call | tf_op jit(solution)/shard_map/volume_gradient/pallas_call | solution.py:462
  93.1 0.0 copy-done.1
  93.1 0.0 copy-done.6
  93.1 1.9 %fusion.1 = f32[2,1,128,2048]{3,2,1,0:T(8,128)} fusion(bf16[2,128,2048]{2,1,0:T(8,128)(2,1)S(1)} %volume_gradient.1, bf16[2,1,128,2048]{3,2,1,0:T(8,128)(2,1)S(1)} %copy-done.6, bf16[2,1,128,2048]{3,2,1,0:T(8,128)(2,1)S(1)} %copy-done.1), kind=kLoop, calls=%fused_computation.3 | loop fusion | flops 4194304 | bytes 5242880 | tf_op jit(solution)/shard_map/sub | solution.py:497
Async XLA Ops:
  0.0 44.5 %copy-start.2 = (bf16[256,256]{1,0:T(8,128)(2,1)S(1)}, bf16[256,256]{1,0:T(8,128)(2,1)}, u32[]{:S(2)}) copy-start(bf16[256,256]{1,0:T(8,128)(2,1)} %constant.9.clone.inverse) | copy-start | bytes 393220
  0.0 44.5 %copy-start.3 = (bf16[256,256]{1,0:T(8,128)(2,1)S(1)}, bf16[256,256]{1,0:T(8,128)(2,1)}, u32[]{:S(2)}) copy-start(bf16[256,256]{1,0:T(8,128)(2,1)} %constant.8.clone.forward) | copy-start | bytes 393220
  0.0 44.5 %copy-start.5 = (s32[1,16]{1,0:T(1,128)S(1)}, s32[1,16]{1,0:T(1,128)}, u32[]{:S(2)}) copy-start(s32[1,16]{1,0:T(1,128)} %param.12) | copy-start | bytes 196
  0.0 44.5 %copy-start.4 = (bf16[2,128,128]{2,1,0:T(8,128)(2,1)S(1)}, bf16[2,128,128]{2,1,0:T(8,128)(2,1)}, u32[]{:S(2)}) copy-start(bf16[2,128,128]{2,1,0:T(8,128)(2,1)} %probe.1) | copy-start | bytes 196612
  1.9 1.2 %copy-start = (bf16[2,1,128,2048]{3,2,1,0:T(8,128)(2,1)S(1)}, bf16[2,1,128,2048]{3,2,1,0:T(8,128)(2,1)}, u32[]{:S(2)}) copy-start(bf16[2,1,128,2048]{3,2,1,0:T(8,128)(2,1)} %param.8) | copy-start | bytes 3145732
  44.6 48.5 %copy-start.1 = (bf16[2,1,128,2048]{3,2,1,0:T(8,128)(2,1)S(1)}, bf16[2,1,128,2048]{3,2,1,0:T(8,128)(2,1)}, u32[]{:S(2)}) copy-start(bf16[2,1,128,2048]{3,2,1,0:T(8,128)(2,1)} %param.8) | copy-start | bytes 3145732
  44.6 48.5 %copy-start.6 = (bf16[2,1,128,2048]{3,2,1,0:T(8,128)(2,1)S(1)}, bf16[2,1,128,2048]{3,2,1,0:T(8,128)(2,1)}, u32[]{:S(2)}) copy-start(bf16[2,1,128,2048]{3,2,1,0:T(8,128)(2,1)} %param.9) | copy-start | bytes 3145732

commit v4 on v3

--- a/solution.py
+++ b/solution.py
@@ -148,10 +148,14 @@
             copy.wait_send()
 
 
+WHOLE = ((1, 0), (0, 7), (0, 1))
+PIECES = ((7, (1,)), (1, (1,)), (2, (0, 1)), (6, (0, 1)), (3, (0, 1)), (5, (0, 1)), (4, (0, 1)))
+
+
 def to_y(here, copies, piece, k, sems):
     send, recv = sems
     mine = piece(here.y)
-    for d in (1, 3, 2):
+    for d in (2, 1, 3):
         copies.start(mine, mine, send.at[d, k], recv.at[NY - d, k], here.angle_peer(0, d))
 
 
@@ -162,45 +166,56 @@
 
 
 def project_kernel(
-    vol, off, proj, offs_out, gath, acc, sib, offt, offv, offs_s,
+    vol, off, proj, offs_out, gath, acc, sib, offt, offv, off_s, offs_s,
     s_off, r_off, s_t1, r_t1, s_y, r_y, s_sib, r_sib, s_z, r_z, s_x, r_x, s_c, r_c, s_oa, r_oa, l_sem,
 ):
     here = Here()
-    offt[here.m] = jnp.full((8, LANES), off[0, 0], jnp.int32)
+    fetch = pltpu.make_async_copy(off, off_s, l_sem.at[2])
+    fetch.start()
     here.greet()
     copies = Copies(here)
     order = (0, 1, 7, 2, 6, 3, 5, 4)
     cols = chunk_cols(here.y)
-    for rel in order:
+
+    def send_block(f, rel, where):
         r = (NZC - rel) % NZC
-        for f in (0, 1):
-            if rel or f:
-                to = here.chip(r, f)
-                block = here.x_of(f) * NZC + here.z_of(r)
-                copies.start(offt.at[here.m], offt.at[here.m], s_off.at[f, rel], r_off.at[f, rel], to)
-                copies.start(
-                    vol.at[rows16(block), cols], gath.at[f, rel, :, cols], s_t1.at[f, rel], r_t1.at[f, rel], to
-                )
+        to = here.chip(r, f)
+        block = here.x_of(f) * NZC + here.z_of(r)
+        copies.start(vol.at[rows16(block), where], gath.at[f, rel, :, where], s_t1.at[f, rel], r_t1.at[f, rel], to)
+
+    for rel, flips in PIECES:
+        for f in flips:
+            send_block(f, rel, cols)
+    for f, rel in WHOLE:
+        send_block(f, rel, slice(None))
     own = pltpu.make_async_copy(vol.at[rows16(here.m)], gath.at[0, 0], l_sem.at[0])
     own.start()
-
-    def piece(rel):
-        if rel == 0:
-            return lambda y: gath.at[1, 0, :, chunk_cols(y)]
-        return lambda y: gath.at[:, rel, :, chunk_cols(y)]
-
+    fetch.wait()
+    offt[here.m] = jnp.full((1, LANES), off_s[0, 0], jnp.int32)
     for rel in order:
         for f in (0, 1):
             if rel or f:
-                copies.arrived(gath.at[f, rel, :, cols], r_t1.at[f, rel])
-        to_y(here, copies, piece(rel), rel, (s_y, r_y))
+                to = here.chip((NZC - rel) % NZC, f)
+                copies.start(offt.at[here.m], offt.at[here.m], s_off.at[f, rel], r_off.at[f, rel], to)
+
+    def piece(rel, flips):
+        f = slice(None) if len(flips) == 2 else flips[0]
+        return lambda y: gath.at[f, rel, :, chunk_cols(y)]
+
+    for rel, flips in PIECES:
+        for f in flips:
+            copies.arrived(gath.at[f, rel, :, cols], r_t1.at[f, rel])
+        to_y(here, copies, piece(rel, flips), rel, (s_y, r_y))
 
     for f in (0, 1):
         for r in range(NZC):
             if r or f:
                 copies.arrived(offt.at[here.x_of(f) * NZC + here.z_of(r)], r_off.at[f, r])
+    lane = lax.broadcasted_iota(jnp.int32, (1, LANES), 1)
+    packed = jnp.zeros((1, LANES), jnp.int32)
     for g in range(NXL * NZC):
-        offv[g : g + 1, :] = offt[g, 0:1, :]
+        packed = jnp.where(lane == g, offt[g], packed)
+    offv[...] = packed
     down = pltpu.make_async_copy(offv, offs_s, l_sem.at[1])
     down.start()
     for f in (0, 1):
@@ -208,20 +223,24 @@
             if r or f:
                 back = (NY - r) % NY
                 copies.start(offv, offs_out.at[here.a], s_oa.at[f, r], r_oa.at[f, back], here.angle_peer(f, r))
-    offs_out[here.a] = offv[...]
+    offs_out[here.a] = packed
     down.wait()
     own.wait()
     acc[...] = jnp.zeros_like(acc)
-    for rel in order:
-        from_y(here, copies, piece(rel), rel, (s_y, r_y))
-
-        def add_slot(f, carry):
-            g = lax.rem(here.xl + f, NXL) * NZC + here.z_of(rel)
-            for j, tile in enumerate(shifted_tiles(tiles_of(gath[f, rel]), offs_s[g, 0], TILES)):
-                acc[:, j * LANES : (j + 1) * LANES] += tile
-            return carry
-
-        lax.fori_loop(0, NXL, add_slot, 0)
+
+    def add_slot(f, rel):
+        g = lax.rem(here.xl + f, NXL) * NZC + here.z_of(rel)
+        for j, tile in enumerate(shifted_tiles(tiles_of(gath[f, rel]), offs_s[0, g], TILES)):
+            acc[:, j * LANES : (j + 1) * LANES] += tile
+
+    add_slot(0, 0)
+    for f, rel in WHOLE:
+        copies.arrived(gath.at[f, rel], r_t1.at[f, rel])
+        add_slot(f, rel)
+    for rel, flips in PIECES:
+        from_y(here, copies, piece(rel, flips), rel, (s_y, r_y))
+        for f in flips:
+            add_slot(f, rel)
 
     mine, other = half_cols(here.c), half_cols(1 - here.c)
     copies.start(acc.at[:, other], sib, s_sib, r_sib, here.sibling)
@@ -370,37 +389,45 @@
     cols = chunk_cols(here.y)
     zrows = rows16(here.zc)
 
-    def gradient(f, r):
-        g = here.x_of(f) * NZC + here.z_of(r)
+    def gradient(f, rel, start, count):
+        g = here.x_of(f) * NZC + here.z_of((NZC - rel) % NZC)
         sums = None
         for b in range(ANGLES):
-            first = (here.y * CHUNK + NX - offs[b * NXL * NZC + g, 0]) & (NX - 1)
-            tiles = shifted_tiles(tiles_of(dgall[b]), first, CHUNK // LANES)
+            first = (start + NX - offs[b, g]) & (NX - 1)
+            tiles = shifted_tiles(tiles_of(dgall[b]), first, count)
             sums = tiles if sums is None else [x + t for x, t in zip(sums, tiles)]
         return jnp.concatenate(sums, axis=1).astype(jnp.bfloat16)
 
-    order = (0, 1, 7, 2, 6, 3, 5, 4)
-    for rel in order:
-        r = (NZC - rel) % NZC
-        for f in (0, 1):
-            if r or f:
-                vsend[f, r] = gradient(f, r)
-                copies.start(
-                    vsend.at[f, r], out.at[here.xl, zrows, cols], s_v.at[f, r], r_v.at[f, rel], here.chip(r, f)
-                )
-            else:
-                out[here.xl, zrows, cols] = gradient(f, r)
-
-    def piece(rel):
-        return lambda y: out.at[:, rows16(here.z_of(rel)), chunk_cols(y)]
-
-    for rel in order:
-        for f in (0, 1):
-            if rel or f:
-                copies.arrived(out.at[here.x_of(f), rows16(here.z_of(rel)), cols], r_v.at[f, rel])
-        to_y(here, copies, piece(rel), rel, (s_y, r_y))
-    for rel in order:
-        from_y(here, copies, piece(rel), rel, (s_y, r_y))
+    def send_block(f, rel, where):
+        copies.start(
+            vsend.at[f, rel, :, where],
+            out.at[here.xl, zrows, where],
+            s_v.at[f, rel],
+            r_v.at[f, rel],
+            here.chip((NZC - rel) % NZC, f),
+        )
+
+    for rel, flips in PIECES:
+        for f in flips:
+            vsend[f, rel, :, cols] = gradient(f, rel, here.y * CHUNK, CHUNK // LANES)
+            send_block(f, rel, cols)
+    for f, rel in WHOLE:
+        vsend[f, rel] = gradient(f, rel, 0, TILES)
+        send_block(f, rel, slice(None))
+    out[here.xl, zrows, :] = gradient(0, 0, 0, TILES)
+
+    def piece(rel, flips):
+        f = slice(None) if len(flips) == 2 else here.x_of(flips[0])
+        return lambda y: out.at[f, rows16(here.z_of(rel)), chunk_cols(y)]
+
+    for rel, flips in PIECES:
+        for f in flips:
+            copies.arrived(out.at[here.x_of(f), rows16(here.z_of(rel)), cols], r_v.at[f, rel])
+        to_y(here, copies, piece(rel, flips), rel, (s_y, r_y))
+    for f, rel in WHOLE:
+        copies.arrived(out.at[here.x_of(f), rows16(here.z_of(rel))], r_v.at[f, rel])
+    for rel, flips in PIECES:
+        from_y(here, copies, piece(rel, flips), rel, (s_y, r_y))
     copies.drain()
 
 
@@ -421,26 +448,27 @@
         project_kernel,
         out_shape=(
             jax.ShapeDtypeStruct((2 * PW, NX), jnp.bfloat16),
-            jax.ShapeDtypeStruct((ANGLES, NXL * NZC, LANES), jnp.int32),
+            jax.ShapeDtypeStruct((ANGLES, 1, LANES), jnp.int32),
         ),
-        in_specs=[vmem(), smem()],
+        in_specs=[pl.BlockSpec(memory_space=pl.ANY), pl.BlockSpec(memory_space=pl.ANY)],
         out_specs=(vmem(), vmem()),
         scratch_shapes=[
             pltpu.VMEM((NXL, NZC, BLOCK, NX), jnp.bfloat16),
             pltpu.VMEM((BLOCK, NX), jnp.float32),
             pltpu.VMEM((BLOCK, HALF), jnp.float32),
-            pltpu.VMEM((NXL * NZC, 8, LANES), jnp.int32),
-            pltpu.VMEM((NXL * NZC, LANES), jnp.int32),
-            pltpu.SMEM((NXL * NZC, LANES), jnp.int32),
+            pltpu.VMEM((NXL * NZC, 1, LANES), jnp.int32),
+            pltpu.VMEM((1, LANES), jnp.int32),
+            pltpu.SMEM((1, 1), jnp.int32),
+            pltpu.SMEM((1, LANES), jnp.int32),
             dma(NXL, NZC), dma(NXL, NZC), dma(NXL, NZC), dma(NXL, NZC),
             dma(NY, NZC), dma(NY, NZC),
             pltpu.SemaphoreType.DMA, pltpu.SemaphoreType.DMA,
             dma(NZC), dma(NZC), dma(NZC), dma(NZC),
             dma(NXL, NZC), dma(NXL, NZC),
             dma(NXH, NY), dma(NXH, NY),
-            dma(2),
+            dma(3),
         ],
-        compiler_params=pltpu.CompilerParams(collective_id=0, has_side_effects=True, vmem_limit_bytes=VMEM),
+        compiler_params=pltpu.CompilerParams(collective_id=0, has_side_effects=True, vmem_limit_bytes=52 * 1024 * 1024),
         name="project",
     )(lines, off)
 
@@ -471,7 +499,7 @@
             pltpu.VMEM((NZC, BLOCK, HALF), bf16),
             pltpu.VMEM((NZC, BLOCK, HALF), bf16),
             pltpu.VMEM((ANGLES, BLOCK, NX), bf16),
-            pltpu.VMEM((NXL, NZC, BLOCK, CHUNK), bf16),
+            pltpu.VMEM((NXL, NZC, BLOCK, NX), bf16),
             dma(NXL, NZC), dma(NXL, NZC),
             dma(NZC), dma(NZC), dma(NZC), dma(NZC),
             dma(NXH, NY), dma(NXH, NY), dma(NXH, NY), dma(NXH, NY),
@@ -490,7 +518,7 @@
     measured = intensities.reshape(PW, pos_count * PW)
     proj, offs = project(lines, offsets)
     part = waves(proj, probe, measured, positions.reshape(-1), jnp.asarray(forward), jnp.asarray(inverse))
-    grad = volume_gradient(part, offs.reshape(ANGLES * NXL * NZC, LANES))
+    grad = volume_gradient(part, offs.reshape(ANGLES, LANES))
     rate = math.sqrt(NX / (pos_count * lax.axis_size("slab") * ANGLES * PW))
     current = volume.astype(jnp.float32)
     step = grad[:, None].astype(jnp.float32)

time: 95.1 us -> 88.9 us (0.935)
  Pallas kernels: 89.9 us -> 84.9 us
  local copies, waits for them, and re-layouts: 2.43 us -> 1.21 us
    pallas_call x1, Pallas kernels: 44.5 us -> 40.5 us  [volume_gradient(): pl.pallas_call(volume_kernel, out_shape=jax.ShapeDtypeStruct((2, PW, NX),...]
    unnamed x15 -> x13, local copies, waits for them, and re-layouts: 2.43 us -> 1.21 us
    pallas_call x1, Pallas kernels: 41.4 us -> 40.4 us  [project(): pl.pallas_call(project_kernel, out_shape=(jax.ShapeDtypeStruct((2 * PW, N...]
where the time goes in v4:
time: 88.9 us; the launch traced here: 88.8 us
  Pallas kernels  84.9 us (96%)
  other arithmetic  1.87 us (2%)
  local copies, waits for them, and re-layouts  1.21 us (1%)
    pallas_call x1, Pallas kernels, volume_gradient(): pl.pallas_call(volume_kernel, out_shape=jax.ShapeDtypeStruct((2, PW, NX),...  40.5 us
    pallas_call x1, Pallas kernels, project(): pl.pallas_call(project_kernel, out_shape=(jax.ShapeDtypeStruct((2 * PW, N...  40.4 us
    pallas_call x1, Pallas kernels, waves(): pl.pallas_call(wave_kernel, out_shape=jax.ShapeDtypeStruct((2 * PW, NX),...  4.01 us
    sub x1, other arithmetic, per_device(): current - rate * step - MIX * (current - consensus.astype(jnp.float32))  1.87 us

profile of v4, /device:TPU:1, one launch (start us, length us, event | category | flops | bytes accessed | tf_op | source)
XLA Modules:
  0.0 88.8 jit_solution(11765876563776195637)
XLA Ops:
  0.0 0.0 copy-start
  0.0 0.0 copy-start.1
  0.0 0.0 copy-start.3
  0.0 0.0 copy-start.2
  0.7 1.2 %copy.14 = bf16[16,8,16,128]{3,1,2,0:T(8,128)(2,1)S(1)} copy(bf16[16,8,16,128]{3,2,1,0:T(8,128)(2,1)} %bitcast.20) | data formatting | bytes 1048576
  1.9 40.4 %project.1 = (bf16[256,2048]{1,0:T(8,128)(2,1)S(1)}, s32[8,1,128]{2,1,0:T(1,128)S(1)}) custom-call(bf16[256,2048]{1,0:T(8,128)(2,1)} %bitcast.19, s32[1,1]{1,0:T(1,128)S(6)} %copy.15.off), custom_call_target="tpu_custom_call" | custom-call | tf_op jit(solution)/shard_map/project/pallas_call | solution.py:447
  42.3 0.0 copy-done
  42.3 0.0 copy-done.1
  42.3 0.0 copy-done.3
  42.3 0.0 copy-done.2
  42.3 0.0 copy-start.4
  42.3 0.0 copy-start.5
  42.3 4.0 %waves.1.part = bf16[256,2048]{1,0:T(8,128)(2,1)S(1)} custom-call(bf16[256,2048]{1,0:T(8,128)(2,1)S(1)} %get-tuple-element.7.proj, bf16[2,128,128]{2,1,0:T(8,128)(2,1)S(1)} %copy-done.2, bf16[128,2048]{1,0:T(8,128)(2,1)S(1)} %bitcast.16, s32[16]{0:T(128)S(1)} %bitcast.18, bf16[256,256]{1,0:T(8,128)(2,1)S(1)} %copy-done.1, bf16[256,256]{1,0:T(8,128)(2,1)S(1)} %copy-done), custom_call_target="tpu_custom_call" | custom-call | tf_op jit(solution)/shard_map/waves/pallas_call | solution.py:477
  46.3 40.5 %volume_gradient.1 = bf16[2,128,2048]{2,1,0:T(8,128)(2,1)S(1)} custom-call(bf16[256,2048]{1,0:T(8,128)(2,1)S(1)} %waves.1.part, s32[8,128]{1,0:T(8,128)S(1)} %bitcast.17), custom_call_target="tpu_custom_call" | custom-call | tf_op jit(solution)/shard_map/volume_gradient/pallas_call | solution.py:490
  86.9 0.0 copy-done.4
  86.9 0.0 copy-done.5
  86.9 1.9 %fusion.1 = f32[2,1,128,2048]{3,2,1,0:T(8,128)} fusion(bf16[2,128,2048]{2,1,0:T(8,128)(2,1)S(1)} %volume_gradient.1, bf16[2,1,128,2048]{3,2,1,0:T(8,128)(2,1)S(1)} %copy-done.5, bf16[2,1,128,2048]{3,2,1,0:T(8,128)(2,1)S(1)} %copy-done.4), kind=kLoop, calls=%fused_computation.3 | loop fusion | flops 4194304 | bytes 5242880 | tf_op jit(solution)/shard_map/sub | solution.py:525
Async XLA Ops:
  0.0 42.3 %copy-start = (bf16[256,256]{1,0:T(8,128)(2,1)S(1)}, bf16[256,256]{1,0:T(8,128)(2,1)}, u32[]{:S(2)}) copy-start(bf16[256,256]{1,0:T(8,128)(2,1)} %constant.9.clone.inverse) | copy-start | bytes 393220
  0.0 42.3 %copy-start.1 = (bf16[256,256]{1,0:T(8,128)(2,1)S(1)}, bf16[256,256]{1,0:T(8,128)(2,1)}, u32[]{:S(2)}) copy-start(bf16[256,256]{1,0:T(8,128)(2,1)} %constant.8.clone.forward) | copy-start | bytes 393220
  0.0 42.3 %copy-start.3 = (s32[1,16]{1,0:T(1,128)S(1)}, s32[1,16]{1,0:T(1,128)}, u32[]{:S(2)}) copy-start(s32[1,16]{1,0:T(1,128)} %param.12) | copy-start | bytes 196
  0.0 42.3 %copy-start.2 = (bf16[2,128,128]{2,1,0:T(8,128)(2,1)S(1)}, bf16[2,128,128]{2,1,0:T(8,128)(2,1)}, u32[]{:S(2)}) copy-start(bf16[2,128,128]{2,1,0:T(8,128)(2,1)} %probe.1) | copy-start | bytes 196612
  42.3 44.6 %copy-start.4 = (bf16[2,1,128,2048]{3,2,1,0:T(8,128)(2,1)S(1)}, bf16[2,1,128,2048]{3,2,1,0:T(8,128)(2,1)}, u32[]{:S(2)}) copy-start(bf16[2,1,128,2048]{3,2,1,0:T(8,128)(2,1)} %param.8) | copy-start | bytes 3145732
  42.3 44.6 %copy-start.5 = (bf16[2,1,128,2048]{3,2,1,0:T(8,128)(2,1)S(1)}, bf16[2,1,128,2048]{3,2,1,0:T(8,128)(2,1)}, u32[]{:S(2)}) copy-start(bf16[2,1,128,2048]{3,2,1,0:T(8,128)(2,1)} %param.9) | copy-start | bytes 3145732

commit v5 on v4

--- a/solution.py
+++ b/solution.py
@@ -1,3 +1,4 @@
+import functools
 import math
 
 import jax
@@ -77,9 +78,9 @@
         return self.device(c=1 - self.c)
 
     def greet(self):
-        peers = [self.sibling]
-        peers += [self.chip(r, f) for f in (0, 1) for r in range(NZC) if r or f]
-        peers += [self.angle_peer(f, r) for f in (0, 1) for r in range(NY) if r or f]
+        peers = [self.chip(r, f) for r in FAR_FIRST for f in (1, 0) if r or f]
+        peers[8:8] = [self.angle_peer(f, r) for f in (1, 0) for r in (2, 1, 3, 0) if r or f]
+        peers.append(self.sibling)
         barrier = pltpu.get_barrier_semaphore()
         for peer in peers:
             pl.semaphore_signal(barrier, 1, device_id=peer, device_id_type=pl.DeviceIdType.MESH)
@@ -120,7 +121,7 @@
         size = len(tiles)
         tiles = [lax.select_n(bit, tiles[j], tiles[(j + stride) % size]) for j in range(keep)]
     back = (LANES - inner) & (LANES - 1)
-    lane = lax.broadcasted_iota(jnp.int32, (BLOCK, LANES), 1)
+    lane = lax.broadcasted_iota(jnp.int32, tiles[0].shape, 1)
     stay = lane < LANES - inner
     turned = [pltpu.roll(tile.astype(jnp.float32), back, 1) for tile in tiles]
     return [jnp.where(stay, turned[j], turned[(j + 1) % need]) for j in range(count)]
@@ -272,7 +273,20 @@
     copies.drain()
 
 
-GROUP = 8
+GROUP = 16
+BATCHES = 2
+LINES = BLOCK // BATCHES
+PACK = HALF // 2
+QUARTER = CHUNK // 2
+
+
+def pack(x):
+    n = x.shape[1] // 2
+    return jnp.concatenate([x[:, :n], x[:, n:]], axis=0)
+
+
+def unpack(x):
+    return jnp.concatenate([x[:LINES], x[LINES:]], axis=1)
 
 
 def wave_kernel(proj, probe, measured, pos, forward, inverse, out, total):
@@ -333,7 +347,11 @@
         return carry
 
     lax.fori_loop(0, count // GROUP, one_group, 0)
-    out[...] = total[...].astype(jnp.bfloat16)
+    for m in range(NXL * NZC):
+        for h in range(BATCHES):
+            for c in range(2):
+                x = total[m * BLOCK + h * LINES : m * BLOCK + (h + 1) * LINES, c * HALF : (c + 1) * HALF]
+                out[h, c, m] = pack(x).astype(jnp.bfloat16)
 
 
 def volume_kernel(
@@ -343,92 +361,126 @@
     here = Here()
     here.greet()
     copies = Copies(here)
-    mine, other = half_cols(here.c), half_cols(1 - here.c)
-    for f in (1, 0):
+    f32 = jnp.float32
+    batches = range(BATCHES)
+
+    def block(f, r):
+        return here.x_of(f) * NZC + here.z_of(r)
+
+    for h in batches:
+        for f in (1, 0):
+            for r in FAR_FIRST:
+                copies.start(
+                    part.at[h, 1 - here.c, block(f, r)], cbuf.at[h, f, r], s_c.at[h, f, r], r_c.at[h, f, r], here.sibling
+                )
+    for h in batches:
         for r in FAR_FIRST:
-            src = part.at[rows16(here.x_of(f) * NZC + here.z_of(r)), other]
-            copies.start(src, cbuf.at[f, r], s_c.at[f, r], r_c.at[f, r], here.sibling)
-    for r in FAR_FIRST:
-        copies.arrived(cbuf.at[1, r], r_c.at[1, r])
-        own = part[rows16(here.x_of(1) * NZC + here.z_of(r)), mine]
-        xsend[r] = (own.astype(jnp.float32) + cbuf[1, r].astype(jnp.float32)).astype(jnp.bfloat16)
-        copies.start(xsend.at[r], xbuf.at[r], s_x.at[r], r_x.at[r], here.chip(0, 1))
-    total = None
-    for r in FAR_FIRST:
-        copies.arrived(cbuf.at[0, r], r_c.at[0, r])
-        own = part[rows16(here.xl * NZC + here.z_of(r)), mine]
-        value = own.astype(jnp.float32) + cbuf[0, r].astype(jnp.float32)
-        copies.arrived(xbuf.at[r], r_x.at[r])
-        value = value + xbuf[r].astype(jnp.float32)
-        if r:
-            zsend[r] = value.astype(jnp.bfloat16)
-            slot = (NZC - r) % NZC
-            copies.start(zsend.at[r], zbuf.at[slot], s_z.at[r], r_z.at[slot], here.chip(r, 0))
-        else:
-            total = value
-    for r in (1, 7, 2, 6, 3, 5, 4):
-        copies.arrived(zbuf.at[r], r_z.at[r])
-        total = total + zbuf[r].astype(jnp.float32)
-    dgall[here.a, :, mine] = total.astype(jnp.bfloat16)
-    own = dgall.at[here.a, :, mine]
+            copies.arrived(cbuf.at[h, 1, r], r_c.at[h, 1, r])
+            value = part[h, here.c, block(1, r)].astype(f32) + cbuf[h, 1, r].astype(f32)
+            xsend[h, r] = value.astype(jnp.bfloat16)
+            copies.start(xsend.at[h, r], xbuf.at[h, r], s_x.at[h, r], r_x.at[h, r], here.chip(0, 1))
+    totals = []
+    for h in batches:
+        for r in FAR_FIRST:
+            copies.arrived(cbuf.at[h, 0, r], r_c.at[h, 0, r])
+            value = part[h, here.c, block(0, r)].astype(f32) + cbuf[h, 0, r].astype(f32)
+            copies.arrived(xbuf.at[h, r], r_x.at[h, r])
+            value = value + xbuf[h, r].astype(f32)
+            if r:
+                zsend[h, r] = value.astype(jnp.bfloat16)
+                slot = (NZC - r) % NZC
+                copies.start(zsend.at[h, r], zbuf.at[h, slot], s_z.at[h, r], r_z.at[h, slot], here.chip(r, 0))
+            else:
+                totals.append(value)
     peers = [(0, 1), (0, 3), (1, 0), (0, 2), (1, 1), (1, 3), (1, 2)]
-    for f, r in peers:
-        copies.start(own, own, s_a.at[f, r], r_a.at[f, (NY - r) % NY], here.angle_peer(f, r))
-    copies.start(own, own, s_s.at[0, 0], r_s.at[0, 0], here.sibling)
+    for h in batches:
+        total = totals[h]
+        for r in (1, 7, 2, 6, 3, 5, 4):
+            copies.arrived(zbuf.at[h, r], r_z.at[h, r])
+            total = total + zbuf[h, r].astype(f32)
+        dgall[h, here.a, here.c] = total.astype(jnp.bfloat16)
+        own = dgall.at[h, here.a, here.c]
+        for f, r in peers:
+            copies.start(own, own, s_a.at[h, f, r], r_a.at[h, f, (NY - r) % NY], here.angle_peer(f, r))
+        copies.start(own, own, s_s.at[h, 0, 0], r_s.at[h, 0, 0], here.sibling)
 
     def angle_of(f, r):
         return (1 - here.xh if f else here.xh) * NY + here.y_of(r)
 
-    for f, r in peers:
-        got = dgall.at[angle_of(f, r), :, mine]
-        copies.arrived(got, r_a.at[f, r])
-        copies.start(got, got, s_s.at[f, r], r_s.at[f, r], here.sibling)
-    for f, r in [(0, 0)] + peers:
-        copies.arrived(dgall.at[angle_of(f, r), :, other], r_s.at[f, r])
-
-    cols = chunk_cols(here.y)
-    zrows = rows16(here.zc)
-
-    def gradient(f, rel, start, count):
+    def gradient(h, f, rel, start, count):
         g = here.x_of(f) * NZC + here.z_of((NZC - rel) % NZC)
         sums = None
         for b in range(ANGLES):
             first = (start + NX - offs[b, g]) & (NX - 1)
-            tiles = shifted_tiles(tiles_of(dgall[b]), first, count)
+            tiles = []
+            for c in range(2):
+                row = unpack(dgall[h, b, c].astype(f32))
+                tiles += [row[:, j * LANES : (j + 1) * LANES] for j in range(TILES // 2)]
+            tiles = shifted_tiles(tiles, first, count)
             sums = tiles if sums is None else [x + t for x, t in zip(sums, tiles)]
-        return jnp.concatenate(sums, axis=1).astype(jnp.bfloat16)
-
-    def send_block(f, rel, where):
-        copies.start(
-            vsend.at[f, rel, :, where],
-            out.at[here.xl, zrows, where],
-            s_v.at[f, rel],
-            r_v.at[f, rel],
-            here.chip((NZC - rel) % NZC, f),
-        )
-
-    for rel, flips in PIECES:
-        for f in flips:
-            vsend[f, rel, :, cols] = gradient(f, rel, here.y * CHUNK, CHUNK // LANES)
-            send_block(f, rel, cols)
-    for f, rel in WHOLE:
-        vsend[f, rel] = gradient(f, rel, 0, TILES)
-        send_block(f, rel, slice(None))
-    out[here.xl, zrows, :] = gradient(0, 0, 0, TILES)
-
-    def piece(rel, flips):
+        return sums
+
+    def quarter(sums):
+        return pack(jnp.concatenate(sums, axis=1)).astype(jnp.bfloat16)
+
+    per = CHUNK // LANES
+
+    def send_block(h, f, rel, src, dst):
+        copies.start(src, dst, s_v.at[h, f, rel], r_v.at[h, f, rel], here.chip((NZC - rel) % NZC, f))
+
+    for h in batches:
+        for f, r in peers:
+            got = dgall.at[h, angle_of(f, r), here.c]
+            copies.arrived(got, r_a.at[h, f, r])
+            copies.start(got, got, s_s.at[h, f, r], r_s.at[h, f, r], here.sibling)
+        for f, r in [(0, 0)] + peers:
+            copies.arrived(dgall.at[h, angle_of(f, r), 1 - here.c], r_s.at[h, f, r])
+        for rel, flips in PIECES:
+            for f in flips:
+                vsend[h, f, rel, here.y] = quarter(gradient(h, f, rel, here.y * CHUNK, per))
+                send_block(h, f, rel, vsend.at[h, f, rel, here.y], out.at[here.xl, here.zc, h, here.y])
+        for f, rel in WHOLE:
+            sums = gradient(h, f, rel, 0, TILES)
+            for y in range(NY):
+                vsend[h, f, rel, y] = quarter(sums[y * per : (y + 1) * per])
+            send_block(h, f, rel, vsend.at[h, f, rel], out.at[here.xl, here.zc, h])
+        sums = gradient(h, 0, 0, 0, TILES)
+        for y in range(NY):
+            out[here.xl, here.zc, h, y] = quarter(sums[y * per : (y + 1) * per])
+
+    def piece(h, rel, flips):
         f = slice(None) if len(flips) == 2 else here.x_of(flips[0])
-        return lambda y: out.at[f, rows16(here.z_of(rel)), chunk_cols(y)]
-
-    for rel, flips in PIECES:
-        for f in flips:
-            copies.arrived(out.at[here.x_of(f), rows16(here.z_of(rel)), cols], r_v.at[f, rel])
-        to_y(here, copies, piece(rel, flips), rel, (s_y, r_y))
-    for f, rel in WHOLE:
-        copies.arrived(out.at[here.x_of(f), rows16(here.z_of(rel))], r_v.at[f, rel])
-    for rel, flips in PIECES:
-        from_y(here, copies, piece(rel, flips), rel, (s_y, r_y))
+        return lambda y: out.at[f, here.z_of(rel), h, y]
+
+    for h in batches:
+        for rel, flips in PIECES:
+            for f in flips:
+                copies.arrived(out.at[here.x_of(f), here.z_of(rel), h, here.y], r_v.at[h, f, rel])
+            to_y(here, copies, piece(h, rel, flips), rel, (s_y.at[h], r_y.at[h]))
+    for h in batches:
+        for f, rel in WHOLE:
+            copies.arrived(out.at[here.x_of(f), here.z_of(rel), h], r_v.at[h, f, rel])
+        for rel, flips in PIECES:
+            from_y(here, copies, piece(h, rel, flips), rel, (s_y.at[h], r_y.at[h]))
     copies.drain()
+
+
+def update_kernel(rate, grad, volume, consensus, out, made, sems):
+    copies = []
+    for m in range(NXL * NZC):
+        rows = slice(m * BLOCK, (m + 1) * BLOCK)
+        current = volume[rows].astype(jnp.float32)
+        kept = current - MIX * (current - consensus[rows].astype(jnp.float32))
+        for h in range(BATCHES):
+            for y in range(NY):
+                step = unpack(grad[m, h, y].astype(jnp.float32))
+                lines = slice(h * LINES, (h + 1) * LINES)
+                cols = slice(y * CHUNK, (y + 1) * CHUNK)
+                made[m * BLOCK + h * LINES : m * BLOCK + (h + 1) * LINES, cols] = kept[lines, cols] - rate * step
+        copies.append(pltpu.make_async_copy(made.at[rows], out.at[rows], sems.at[m]))
+        copies[-1].start()
+    for copy in copies:
+        copy.wait()
 
 
 def dma(*shape):
@@ -476,7 +528,7 @@
 def waves(proj, probe, measured, pos, forward, inverse):
     return pl.pallas_call(
         wave_kernel,
-        out_shape=jax.ShapeDtypeStruct((2 * PW, NX), jnp.bfloat16),
+        out_shape=jax.ShapeDtypeStruct((BATCHES, 2, NXL * NZC, BLOCK, PACK), jnp.bfloat16),
         in_specs=[vmem(), vmem(), vmem(), smem(), vmem(), vmem()],
         out_specs=vmem(),
         scratch_shapes=[pltpu.VMEM((2 * PW, NX), jnp.float32)],
@@ -487,28 +539,42 @@
 
 def volume_gradient(part, offs):
     bf16 = jnp.bfloat16
+    small = (BATCHES, NZC, BLOCK, PACK)
     return pl.pallas_call(
         volume_kernel,
-        out_shape=jax.ShapeDtypeStruct((2, PW, NX), bf16),
+        out_shape=jax.ShapeDtypeStruct((NXL, NZC, BATCHES, NY, BLOCK, QUARTER), bf16),
         in_specs=[vmem(), smem()],
         out_specs=vmem(),
         scratch_shapes=[
-            pltpu.VMEM((NXL, NZC, BLOCK, HALF), bf16),
-            pltpu.VMEM((NZC, BLOCK, HALF), bf16),
-            pltpu.VMEM((NZC, BLOCK, HALF), bf16),
-            pltpu.VMEM((NZC, BLOCK, HALF), bf16),
-            pltpu.VMEM((NZC, BLOCK, HALF), bf16),
-            pltpu.VMEM((ANGLES, BLOCK, NX), bf16),
-            pltpu.VMEM((NXL, NZC, BLOCK, NX), bf16),
-            dma(NXL, NZC), dma(NXL, NZC),
-            dma(NZC), dma(NZC), dma(NZC), dma(NZC),
-            dma(NXH, NY), dma(NXH, NY), dma(NXH, NY), dma(NXH, NY),
-            dma(NXL, NZC), dma(NXL, NZC),
-            dma(NY, NZC), dma(NY, NZC),
+            pltpu.VMEM((BATCHES, NXL, NZC, BLOCK, PACK), bf16),
+            pltpu.VMEM(small, bf16),
+            pltpu.VMEM(small, bf16),
+            pltpu.VMEM(small, bf16),
+            pltpu.VMEM(small, bf16),
+            pltpu.VMEM((BATCHES, ANGLES, 2, BLOCK, PACK), bf16),
+            pltpu.VMEM((BATCHES, NXL, NZC, NY, BLOCK, QUARTER), bf16),
+            dma(BATCHES, NXL, NZC), dma(BATCHES, NXL, NZC),
+            dma(BATCHES, NZC), dma(BATCHES, NZC), dma(BATCHES, NZC), dma(BATCHES, NZC),
+            dma(BATCHES, NXH, NY), dma(BATCHES, NXH, NY), dma(BATCHES, NXH, NY), dma(BATCHES, NXH, NY),
+            dma(BATCHES, NXL, NZC), dma(BATCHES, NXL, NZC),
+            dma(BATCHES, NY, NZC), dma(BATCHES, NY, NZC),
         ],
         compiler_params=pltpu.CompilerParams(collective_id=1, has_side_effects=True, vmem_limit_bytes=VMEM),
+        cost_estimate=pl.CostEstimate(flops=10**8, bytes_accessed=10**8, transcendentals=0),
         name="volume_gradient",
     )(part, offs)
+
+
+def update(rate, grad, lines, consensus):
+    return pl.pallas_call(
+        functools.partial(update_kernel, rate),
+        out_shape=jax.ShapeDtypeStruct((2 * PW, NX), jnp.float32),
+        in_specs=[vmem(), vmem(), vmem()],
+        out_specs=pl.BlockSpec(memory_space=pl.ANY),
+        scratch_shapes=[pltpu.VMEM((2 * PW, NX), jnp.float32), dma(NXL * NZC)],
+        compiler_params=pltpu.CompilerParams(vmem_limit_bytes=VMEM),
+        name="update",
+    )(grad, lines, consensus)
 
 
 def per_device(volume, consensus, probe, intensities, positions, offsets):
@@ -520,9 +586,8 @@
     part = waves(proj, probe, measured, positions.reshape(-1), jnp.asarray(forward), jnp.asarray(inverse))
     grad = volume_gradient(part, offs.reshape(ANGLES, LANES))
     rate = math.sqrt(NX / (pos_count * lax.axis_size("slab") * ANGLES * PW))
-    current = volume.astype(jnp.float32)
-    step = grad[:, None].astype(jnp.float32)
-    return current - rate * step - MIX * (current - consensus.astype(jnp.float32))
+    grad = grad.reshape(NXL * NZC, BATCHES, NY, BLOCK, QUARTER)
+    return update(rate, grad, lines, consensus.reshape(2 * PW, NX)).reshape(volume.shape)
 
 
 def solution(mesh):

time: 88.9 us -> 86.4 us (0.972)
  other arithmetic: 1.87 us -> 0 us
    sub x1 -> x0, other arithmetic: 1.87 us -> none  [per_device(): current - rate * step - MIX * (current - consensus.astype(jnp.float32))]
    pallas_call x2 -> x3, Pallas kernels: 44.5 us -> 44.7 us  [the longest x1 39.6 us: volume_gradient(): pl.pallas_call(volume_kernel, out_shape=jax.ShapeDtypeStruct((NXL, NZC, B...]
where the time goes in v5:
time: 86.4 us; the launch traced here: 86.3 us
  Pallas kernels  84.3 us (98%)
  local copies, waits for them, and re-layouts  1.21 us (1%)
    pallas_call x1, Pallas kernels, project(): pl.pallas_call(project_kernel, out_shape=(jax.ShapeDtypeStruct((2 * PW, N...  39.6 us
    pallas_call x1, Pallas kernels, volume_gradient(): pl.pallas_call(volume_kernel, out_shape=jax.ShapeDtypeStruct((NXL, NZC, B...  39.6 us
    pallas_call x1, Pallas kernels, waves(): pl.pallas_call(wave_kernel, out_shape=jax.ShapeDtypeStruct((BATCHES, 2, N...  3.61 us

profile of v5, /device:TPU:1, one launch (start us, length us, event | category | flops | bytes accessed | tf_op | source)
XLA Modules:
  0.0 86.3 jit_solution(6463234173898637743)
XLA Ops:
  0.0 0.0 copy-start.2
  0.0 0.0 copy-start.3
  0.0 0.0 copy-start.5
  0.0 0.0 copy-start.4
  0.7 1.2 %copy.12 = bf16[16,8,16,128]{3,1,2,0:T(8,128)(2,1)S(1)} copy(bf16[16,8,16,128]{3,2,1,0:T(8,128)(2,1)} %bitcast.20) | data formatting | bytes 1048576
  1.9 39.6 %project.1 = (bf16[256,2048]{1,0:T(8,128)(2,1)S(1)}, s32[8,1,128]{2,1,0:T(1,128)S(1)}) custom-call(bf16[256,2048]{1,0:T(8,128)(2,1)} %bitcast.13, s32[1,1]{1,0:T(1,128)S(6)} %copy.13.off), custom_call_target="tpu_custom_call" | custom-call | tf_op jit(solution)/shard_map/project/pallas_call | solution.py:499
  41.5 0.0 copy-done.2
  41.6 0.0 copy-done.3
  41.6 0.0 copy-done.5
  41.6 0.0 copy-done.4
  41.6 0.0 copy-start
  41.6 0.0 copy-start.1
  41.6 3.6 %waves.1.part = bf16[2,2,16,16,512]{4,3,2,1,0:T(8,128)(2,1)S(1)} custom-call(bf16[256,2048]{1,0:T(8,128)(2,1)S(1)} %get-tuple-element.7.proj, bf16[2,128,128]{2,1,0:T(8,128)(2,1)S(1)} %copy-done.4, bf16[128,2048]{1,0:T(8,128)(2,1)S(1)} %bitcast.16, s32[16]{0:T(128)S(1)} %bitcast.19, bf16[256,256]{1,0:T(8,128)(2,1)S(1)} %copy-done.3, ...), custom_call_target="tpu_custom_call" | custom-call | tf_op jit(solution)/shard_map/waves/pallas_call | solution.py:529
  45.2 39.6 %volume_gradient.1 = bf16[2,8,2,4,16,256]{5,4,3,2,1,0:T(8,128)(2,1)S(1)} custom-call(bf16[2,2,16,16,512]{4,3,2,1,0:T(8,128)(2,1)S(1)} %waves.1.part, s32[8,128]{1,0:T(8,128)S(1)} %bitcast.18), custom_call_target="tpu_custom_call" | custom-call | flops 100000000 | bytes 100000000 | tf_op jit(solution)/shard_map/volume_gradient/pallas_call | solution.py:543
  84.8 0.0 copy-done
  84.8 0.0 copy-done.1
  84.8 1.5 %update.1 = f32[256,2048]{1,0:T(8,128)} custom-call(bf16[16,2,4,16,256]{4,3,2,1,0:T(8,128)(2,1)S(1)} %bitcast.15, bf16[256,2048]{1,0:T(8,128)(2,1)S(1)} %bitcast.14, bf16[256,2048]{1,0:T(8,128)(2,1)S(1)} %bitcast.17), custom_call_target="tpu_custom_call" | custom-call | tf_op jit(solution)/shard_map/update/pallas_call | solution.py:569
Async XLA Ops:
  0.0 41.6 %copy-start.2 = (bf16[256,256]{1,0:T(8,128)(2,1)S(1)}, bf16[256,256]{1,0:T(8,128)(2,1)}, u32[]{:S(2)}) copy-start(bf16[256,256]{1,0:T(8,128)(2,1)} %constant.5.clone.inverse) | copy-start | bytes 393220
  0.0 41.6 %copy-start.3 = (bf16[256,256]{1,0:T(8,128)(2,1)S(1)}, bf16[256,256]{1,0:T(8,128)(2,1)}, u32[]{:S(2)}) copy-start(bf16[256,256]{1,0:T(8,128)(2,1)} %constant.4.clone.forward) | copy-start | bytes 393220
  0.0 41.6 %copy-start.5 = (s32[1,16]{1,0:T(1,128)S(1)}, s32[1,16]{1,0:T(1,128)}, u32[]{:S(2)}) copy-start(s32[1,16]{1,0:T(1,128)} %param.12) | copy-start | bytes 196
  0.0 41.6 %copy-start.4 = (bf16[2,128,128]{2,1,0:T(8,128)(2,1)S(1)}, bf16[2,128,128]{2,1,0:T(8,128)(2,1)}, u32[]{:S(2)}) copy-start(bf16[2,128,128]{2,1,0:T(8,128)(2,1)} %probe.1) | copy-start | bytes 196612
  41.6 43.2 %copy-start = (bf16[2,1,128,2048]{3,2,1,0:T(8,128)(2,1)S(1)}, bf16[2,1,128,2048]{3,2,1,0:T(8,128)(2,1)}, u32[]{:S(2)}) copy-start(bf16[2,1,128,2048]{3,2,1,0:T(8,128)(2,1)} %param.8) | copy-start | bytes 3145732
  41.6 43.2 %copy-start.1 = (bf16[2,1,128,2048]{3,2,1,0:T(8,128)(2,1)S(1)}, bf16[2,1,128,2048]{3,2,1,0:T(8,128)(2,1)}, u32[]{:S(2)}) copy-start(bf16[2,1,128,2048]{3,2,1,0:T(8,128)(2,1)} %param.9) | copy-start | bytes 3145732

commit v6 on v5

--- a/solution.py
+++ b/solution.py
@@ -149,8 +149,9 @@
             copy.wait_send()
 
 
-WHOLE = ((1, 0), (0, 7), (0, 1))
-PIECES = ((7, (1,)), (1, (1,)), (2, (0, 1)), (6, (0, 1)), (3, (0, 1)), (5, (0, 1)), (4, (0, 1)))
+WHOLE = ((1, 0), (0, 7), (0, 1), (1, 7), (1, 1))
+PIECES = ((2, (0, 1)), (6, (0, 1)), (3, (0, 1)), (5, (0, 1)), (4, (0, 1)))
+FWD = (0,)
 
 
 def to_y(here, copies, piece, k, sems):
@@ -452,16 +453,26 @@
         f = slice(None) if len(flips) == 2 else here.x_of(flips[0])
         return lambda y: out.at[f, here.z_of(rel), h, y]
 
+    up, dn = here.angle_peer(0, 1), here.angle_peer(0, NY - 1)
     for h in batches:
         for rel, flips in PIECES:
             for f in flips:
                 copies.arrived(out.at[here.x_of(f), here.z_of(rel), h, here.y], r_v.at[h, f, rel])
-            to_y(here, copies, piece(h, rel, flips), rel, (s_y.at[h], r_y.at[h]))
+            mine = piece(h, rel, flips)(here.y)
+            for d in (1, 3) if h in FWD else (2, 1, 3):
+                copies.start(mine, mine, s_y.at[h, d, rel], r_y.at[h, NY - d, rel], here.angle_peer(0, d))
+    for h in FWD:
+        for k, (rel, flips) in enumerate(PIECES):
+            d, to = ((3, up), (1, dn))[k % 2]
+            got = piece(h, rel, flips)(here.y_of(d))
+            copies.arrived(got, r_y.at[h, d, rel])
+            copies.start(got, got, s_y.at[h, 2, rel], r_y.at[h, 2, rel], to)
     for h in batches:
         for f, rel in WHOLE:
             copies.arrived(out.at[here.x_of(f), here.z_of(rel), h], r_v.at[h, f, rel])
-        for rel, flips in PIECES:
-            from_y(here, copies, piece(h, rel, flips), rel, (s_y.at[h], r_y.at[h]))
+        for k, (rel, flips) in enumerate(PIECES):
+            for d in (((1, 2), (3, 2))[k % 2]) if h in FWD else (1, 3, 2):
+                copies.arrived(piece(h, rel, flips)(here.y_of(d)), r_y.at[h, d, rel])
     copies.drain()
 
 

time: 86.4 us -> 85.2 us (0.986)
  Pallas kernels: 84.3 us -> 82.9 us
    pallas_call x1, Pallas kernels: 39.6 us -> 38.6 us  [volume_gradient(): pl.pallas_call(volume_kernel, out_shape=jax.ShapeDtypeStruct((NXL, NZC, B...]
where the time goes in v6:
time: 85.2 us; the launch traced here: 84.9 us
  Pallas kernels  82.9 us (97%)
  local copies, waits for them, and re-layouts  1.21 us (1%)
    pallas_call x1, Pallas kernels, project(): pl.pallas_call(project_kernel, out_shape=(jax.ShapeDtypeStruct((2 * PW, N...  39.2 us
    pallas_call x1, Pallas kernels, volume_gradient(): pl.pallas_call(volume_kernel, out_shape=jax.ShapeDtypeStruct((NXL, NZC, B...  38.6 us
    pallas_call x1, Pallas kernels, waves(): pl.pallas_call(wave_kernel, out_shape=jax.ShapeDtypeStruct((BATCHES, 2, N...  3.61 us

profile of v6, /device:TPU:1, one launch (start us, length us, event | category | flops | bytes accessed | tf_op | source)
XLA Modules:
  0.0 84.9 jit_solution(14840024417126260009)
XLA Ops:
  0.0 0.0 copy-start.2
  0.0 0.0 copy-start.3
  0.0 0.0 copy-start.5
  0.0 0.0 copy-start.4
  0.7 1.2 %copy.12 = bf16[16,8,16,128]{3,1,2,0:T(8,128)(2,1)S(1)} copy(bf16[16,8,16,128]{3,2,1,0:T(8,128)(2,1)} %bitcast.20) | data formatting | bytes 1048576
  1.9 39.2 %project.1 = (bf16[256,2048]{1,0:T(8,128)(2,1)S(1)}, s32[8,1,128]{2,1,0:T(1,128)S(1)}) custom-call(bf16[256,2048]{1,0:T(8,128)(2,1)} %bitcast.13, s32[1,1]{1,0:T(1,128)S(6)} %copy.13.off), custom_call_target="tpu_custom_call" | custom-call | tf_op jit(solution)/shard_map/project/pallas_call | solution.py:510
  41.1 0.0 copy-done.2
  41.1 0.0 copy-done.3
  41.1 0.0 copy-done.5
  41.1 0.0 copy-done.4
  41.1 0.0 copy-start
  41.2 0.0 copy-start.1
  41.2 3.6 %waves.1.part = bf16[2,2,16,16,512]{4,3,2,1,0:T(8,128)(2,1)S(1)} custom-call(bf16[256,2048]{1,0:T(8,128)(2,1)S(1)} %get-tuple-element.7.proj, bf16[2,128,128]{2,1,0:T(8,128)(2,1)S(1)} %copy-done.4, bf16[128,2048]{1,0:T(8,128)(2,1)S(1)} %bitcast.16, s32[16]{0:T(128)S(1)} %bitcast.19, bf16[256,256]{1,0:T(8,128)(2,1)S(1)} %copy-done.3, ...), custom_call_target="tpu_custom_call" | custom-call | tf_op jit(solution)/shard_map/waves/pallas_call | solution.py:540
  44.8 38.6 %volume_gradient.1 = bf16[2,8,2,4,16,256]{5,4,3,2,1,0:T(8,128)(2,1)S(1)} custom-call(bf16[2,2,16,16,512]{4,3,2,1,0:T(8,128)(2,1)S(1)} %waves.1.part, s32[8,128]{1,0:T(8,128)S(1)} %bitcast.18), custom_call_target="tpu_custom_call" | custom-call | flops 100000000 | bytes 100000000 | tf_op jit(solution)/shard_map/volume_gradient/pallas_call | solution.py:554
  83.4 0.0 copy-done
  83.4 0.0 copy-done.1
  83.4 1.5 %update.1 = f32[256,2048]{1,0:T(8,128)} custom-call(bf16[16,2,4,16,256]{4,3,2,1,0:T(8,128)(2,1)S(1)} %bitcast.15, bf16[256,2048]{1,0:T(8,128)(2,1)S(1)} %bitcast.14, bf16[256,2048]{1,0:T(8,128)(2,1)S(1)} %bitcast.17), custom_call_target="tpu_custom_call" | custom-call | tf_op jit(solution)/shard_map/update/pallas_call | solution.py:580
Async XLA Ops:
  0.0 41.1 %copy-start.2 = (bf16[256,256]{1,0:T(8,128)(2,1)S(1)}, bf16[256,256]{1,0:T(8,128)(2,1)}, u32[]{:S(2)}) copy-start(bf16[256,256]{1,0:T(8,128)(2,1)} %constant.5.clone.inverse) | copy-start | bytes 393220
  0.0 41.1 %copy-start.3 = (bf16[256,256]{1,0:T(8,128)(2,1)S(1)}, bf16[256,256]{1,0:T(8,128)(2,1)}, u32[]{:S(2)}) copy-start(bf16[256,256]{1,0:T(8,128)(2,1)} %constant.4.clone.forward) | copy-start | bytes 393220
  0.0 41.1 %copy-start.5 = (s32[1,16]{1,0:T(1,128)S(1)}, s32[1,16]{1,0:T(1,128)}, u32[]{:S(2)}) copy-start(s32[1,16]{1,0:T(1,128)} %param.12) | copy-start | bytes 196
  0.0 41.1 %copy-start.4 = (bf16[2,128,128]{2,1,0:T(8,128)(2,1)S(1)}, bf16[2,128,128]{2,1,0:T(8,128)(2,1)}, u32[]{:S(2)}) copy-start(bf16[2,128,128]{2,1,0:T(8,128)(2,1)} %probe.1) | copy-start | bytes 196612
  41.1 42.2 %copy-start = (bf16[2,1,128,2048]{3,2,1,0:T(8,128)(2,1)S(1)}, bf16[2,1,128,2048]{3,2,1,0:T(8,128)(2,1)}, u32[]{:S(2)}) copy-start(bf16[2,1,128,2048]{3,2,1,0:T(8,128)(2,1)} %param.8) | copy-start | bytes 3145732
  41.2 42.2 %copy-start.1 = (bf16[2,1,128,2048]{3,2,1,0:T(8,128)(2,1)S(1)}, bf16[2,1,128,2048]{3,2,1,0:T(8,128)(2,1)}, u32[]{:S(2)}) copy-start(bf16[2,1,128,2048]{3,2,1,0:T(8,128)(2,1)} %param.9) | copy-start | bytes 3145732

commit v7 on v6

--- a/solution.py
+++ b/solution.py
@@ -254,15 +254,28 @@
         copies.start(own, own, s_z.at[r], r_z.at[(NZC - r) % NZC], here.chip(r, 0))
     copies.start(own, own, s_x.at[0], r_x.at[0], here.chip(0, 1))
     copies.start(own, own, s_c.at[0, 0], r_c.at[0, 0], here.sibling)
+
+    def along(rel):
+        return proj.at[rows16(here.xl * NZC + here.z_of(rel)), mine]
+
+    def across(rel):
+        return proj.at[rows16(here.x_of(1) * NZC + here.z_of(rel)), mine]
+
+    def take(f, rel, got, recv):
+        copies.arrived(got, recv.at[rel])
+        copies.start(got, got, s_c.at[f, rel], r_c.at[f, rel], here.sibling)
+
+    for rel in (1, 7):
+        take(0, rel, along(rel), r_z)
+    take(1, 0, across(0), r_x)
+    for r in (1, 7):
+        copies.start(across(0), across(0), s_x.at[r], r_x.at[NZC - r], here.chip(r, 0))
+    for rel in (2, 6, 3, 5, 4):
+        copies.arrived(along(rel), r_z.at[rel])
+        copies.start(along(rel), along(rel), s_x.at[rel], r_x.at[rel], here.chip(0, 1))
+        copies.start(along(rel), along(rel), s_c.at[0, rel], r_c.at[0, rel], here.sibling)
     for rel in (1, 7, 2, 6, 3, 5, 4):
-        got = proj.at[rows16(here.xl * NZC + here.z_of(rel)), mine]
-        copies.arrived(got, r_z.at[rel])
-        copies.start(got, got, s_x.at[rel], r_x.at[rel], here.chip(0, 1))
-        copies.start(got, got, s_c.at[0, rel], r_c.at[0, rel], here.sibling)
-    for rel in order:
-        got = proj.at[rows16(here.x_of(1) * NZC + here.z_of(rel)), mine]
-        copies.arrived(got, r_x.at[rel])
-        copies.start(got, got, s_c.at[1, rel], r_c.at[1, rel], here.sibling)
+        take(1, rel, across(rel), r_x)
     for f in (0, 1):
         for rel in order:
             copies.arrived(proj.at[rows16(here.x_of(f) * NZC + here.z_of(rel)), other], r_c.at[f, rel])
@@ -401,7 +414,7 @@
             total = total + zbuf[h, r].astype(f32)
         dgall[h, here.a, here.c] = total.astype(jnp.bfloat16)
         own = dgall.at[h, here.a, here.c]
-        for f, r in peers:
+        for f, r in reversed(peers):
             copies.start(own, own, s_a.at[h, f, r], r_a.at[h, f, (NY - r) % NY], here.angle_peer(f, r))
         copies.start(own, own, s_s.at[h, 0, 0], r_s.at[h, 0, 0], here.sibling)
 

time: 85.2 us -> 85.3 us (level)
    pallas_call x1, Pallas kernels: 38.6 us -> 39.5 us  [volume_gradient(): pl.pallas_call(volume_kernel, out_shape=jax.ShapeDtypeStruct((NXL, NZC, B...]
where the time goes in v7:
time: 85.3 us
  Pallas kernels  83.3 us (98%)
  local copies, waits for them, and re-layouts  1.21 us (1%)
    pallas_call x1, Pallas kernels, volume_gradient(): pl.pallas_call(volume_kernel, out_shape=jax.ShapeDtypeStruct((NXL, NZC, B...  39.5 us
    pallas_call x1, Pallas kernels, project(): pl.pallas_call(project_kernel, out_shape=(jax.ShapeDtypeStruct((2 * PW, N...  38.7 us
    pallas_call x1, Pallas kernels, waves(): pl.pallas_call(wave_kernel, out_shape=jax.ShapeDtypeStruct((BATCHES, 2, N...  3.6 us

profile of v7, /device:TPU:1, one launch (start us, length us, event | category | flops | bytes accessed | tf_op | source)
XLA Modules:
  0.0 85.3 jit_solution(12692023894113132884)
XLA Ops:
  0.0 0.0 copy-start.2
  0.0 0.0 copy-start.3
  0.0 0.0 copy-start.5
  0.0 0.0 copy-start.4
  0.7 1.2 %copy.12 = bf16[16,8,16,128]{3,1,2,0:T(8,128)(2,1)S(1)} copy(bf16[16,8,16,128]{3,2,1,0:T(8,128)(2,1)} %bitcast.20) | data formatting | bytes 1048576
  1.9 38.7 %project.1 = (bf16[256,2048]{1,0:T(8,128)(2,1)S(1)}, s32[8,1,128]{2,1,0:T(1,128)S(1)}) custom-call(bf16[256,2048]{1,0:T(8,128)(2,1)} %bitcast.13, s32[1,1]{1,0:T(1,128)S(6)} %copy.13.off), custom_call_target="tpu_custom_call" | custom-call | tf_op jit(solution)/shard_map/project/pallas_call | solution.py:523
  40.6 0.0 copy-done.2
  40.6 0.0 copy-done.3
  40.6 0.0 copy-done.5
  40.7 0.0 copy-done.4
  40.7 0.0 copy-start
  40.7 0.0 copy-start.1
  40.7 3.6 %waves.1.part = bf16[2,2,16,16,512]{4,3,2,1,0:T(8,128)(2,1)S(1)} custom-call(bf16[256,2048]{1,0:T(8,128)(2,1)S(1)} %get-tuple-element.7.proj, bf16[2,128,128]{2,1,0:T(8,128)(2,1)S(1)} %copy-done.4, bf16[128,2048]{1,0:T(8,128)(2,1)S(1)} %bitcast.16, s32[16]{0:T(128)S(1)} %bitcast.19, bf16[256,256]{1,0:T(8,128)(2,1)S(1)} %copy-done.3, ...), custom_call_target="tpu_custom_call" | custom-call | tf_op jit(solution)/shard_map/waves/pallas_call | solution.py:553
  44.3 39.5 %volume_gradient.1 = bf16[2,8,2,4,16,256]{5,4,3,2,1,0:T(8,128)(2,1)S(1)} custom-call(bf16[2,2,16,16,512]{4,3,2,1,0:T(8,128)(2,1)S(1)} %waves.1.part, s32[8,128]{1,0:T(8,128)S(1)} %bitcast.18), custom_call_target="tpu_custom_call" | custom-call | flops 100000000 | bytes 100000000 | tf_op jit(solution)/shard_map/volume_gradient/pallas_call | solution.py:567
  83.8 0.0 copy-done
  83.8 0.0 copy-done.1
  83.8 1.5 %update.1 = f32[256,2048]{1,0:T(8,128)} custom-call(bf16[16,2,4,16,256]{4,3,2,1,0:T(8,128)(2,1)S(1)} %bitcast.15, bf16[256,2048]{1,0:T(8,128)(2,1)S(1)} %bitcast.14, bf16[256,2048]{1,0:T(8,128)(2,1)S(1)} %bitcast.17), custom_call_target="tpu_custom_call" | custom-call | tf_op jit(solution)/shard_map/update/pallas_call | solution.py:593
Async XLA Ops:
  0.0 40.6 %copy-start.2 = (bf16[256,256]{1,0:T(8,128)(2,1)S(1)}, bf16[256,256]{1,0:T(8,128)(2,1)}, u32[]{:S(2)}) copy-start(bf16[256,256]{1,0:T(8,128)(2,1)} %constant.5.clone.inverse) | copy-start | bytes 393220
  0.0 40.6 %copy-start.3 = (bf16[256,256]{1,0:T(8,128)(2,1)S(1)}, bf16[256,256]{1,0:T(8,128)(2,1)}, u32[]{:S(2)}) copy-start(bf16[256,256]{1,0:T(8,128)(2,1)} %constant.4.clone.forward) | copy-start | bytes 393220
  0.0 40.6 %copy-start.5 = (s32[1,16]{1,0:T(1,128)S(1)}, s32[1,16]{1,0:T(1,128)}, u32[]{:S(2)}) copy-start(s32[1,16]{1,0:T(1,128)} %param.12) | copy-start | bytes 196
  0.0 40.7 %copy-start.4 = (bf16[2,128,128]{2,1,0:T(8,128)(2,1)S(1)}, bf16[2,128,128]{2,1,0:T(8,128)(2,1)}, u32[]{:S(2)}) copy-start(bf16[2,128,128]{2,1,0:T(8,128)(2,1)} %probe.1) | copy-start | bytes 196612
  40.7 43.1 %copy-start = (bf16[2,1,128,2048]{3,2,1,0:T(8,128)(2,1)S(1)}, bf16[2,1,128,2048]{3,2,1,0:T(8,128)(2,1)}, u32[]{:S(2)}) copy-start(bf16[2,1,128,2048]{3,2,1,0:T(8,128)(2,1)} %param.8) | copy-start | bytes 3145732
  40.7 43.1 %copy-start.1 = (bf16[2,1,128,2048]{3,2,1,0:T(8,128)(2,1)S(1)}, bf16[2,1,128,2048]{3,2,1,0:T(8,128)(2,1)}, u32[]{:S(2)}) copy-start(bf16[2,1,128,2048]{3,2,1,0:T(8,128)(2,1)} %param.9) | copy-start | bytes 3145732
